TPU v7x, 32 devices: a whole 2x2x4 slice. The times are simulated.
32 devices in a mesh: mode: 2 (over x), slab: 16 (over z, y, core).
Axes of the slice: x: 2, y: 2, z: 4, core: 2. Of those that a mesh axis runs over, the one named last changes fastest.
Arguments:
- log_cond: float32 [64, 128, 128], P('slab'), may hold values from -1 to 1
- head_slope: float32 [64, 128, 128], P('slab'), may hold values from -6 to 6
- modes: bfloat16 [64, 64, 128, 128], P('mode', 'slab'), may hold values from -6 to 6
- obs_cells: int32 [16384], P('slab'), may hold values from 0 to 65535
- obs_var: float32 [16384], P('slab'), may hold values from 0.2 to 2
- misfit: float32 [16384, 16], P('slab'), may hold values from -24 to 24
- base_fields: bfloat16 [16, 64, 128, 128], P(None, 'slab', 'mode'), may hold values from -6 to 6
Outputs:
- fields: float32 [16, 64, 128, 128], P(None, 'slab', 'mode')
Inputs may be any that keep to these rules, and one draw needn't show every extreme that they name: `obs_cells`: entry o names a cell of the planes (o // 1024) * 4 to (o // 1024 + 1) * 4 - 1, counted from the first of them: value c stands for plane (o // 1024) * 4 + c // 16384, first horizontal index (c // 128) % 128, second c % 128; cells may repeat.
All inputs are finite; a program needn't handle non-finite values.
Results may differ from a plain program's by a relative error of at most 0.0003.
Values may be sent and summed in bfloat16 or wider, within the bound.
A program may use at most 128 MiB of HBM per device.

v0:
```python
import math

import jax
import jax.numpy as jnp
from jax import lax
from jax.sharding import PartitionSpec as P

ITERS = 3


STORAGE = 0.05


def padded_2(cells, sides, width):
    for axis, dim in sides:
        count = lax.axis_size(axis)
        ends = count - 1
        head = lax.slice_in_dim(cells, 0, width, axis=dim)
        tail = lax.slice_in_dim(cells, cells.shape[dim] - width, cells.shape[dim], axis=dim)
        cells = jnp.concatenate(
            [
                lax.ppermute(tail, axis, [(i, (i + 1) % count) for i in range(ends)]),
                cells,
                lax.ppermute(head, axis, [((i + 1) % count, i) for i in range(ends)]),
            ],
            axis=dim,
        )
    return cells


def sweep_weights(count):
    order = []
    low, high = (0, count - 1)
    while low <= high:
        order.append(low)
        if high != low:
            order.append(high)
        low += 1
        high -= 1
    return [1.0 / (1.15 + 0.85 * math.cos((2 * i + 1) * math.pi / (2 * count))) for i in order]


def coefficients(cond_ext):
    padded = jnp.pad(cond_ext, ((0, 0), (1, 1), (1, 1)), mode="edge")
    centre = padded[1:-1, 1:-1, 1:-1]

    def harmonic(other):
        return 2.0 * centre * other / (centre + other)

    lower = harmonic(padded[:-2, 1:-1, 1:-1])
    upper = harmonic(padded[2:, 1:-1, 1:-1])
    west = harmonic(padded[1:-1, :-2, 1:-1])
    east = harmonic(padded[1:-1, 2:, 1:-1])
    south = harmonic(padded[1:-1, 1:-1, :-2])
    north = harmonic(padded[1:-1, 1:-1, 2:])
    diag = STORAGE + lower + upper + west + east + south + north
    return (lower, upper, west, east, south, north, diag)


def relax(u_ext, source, coeffs, weight):
    lower, upper, west, east, south, north, diag = coeffs
    core = u_ext[:, 1:-1]
    px = jnp.pad(core, ((0, 0), (0, 0), (1, 1), (0, 0)))
    py = jnp.pad(core, ((0, 0), (0, 0), (0, 0), (1, 1)))
    beside = (
        lower * u_ext[:, :-2]
        + upper * u_ext[:, 2:]
        + west * px[:, :, :-2]
        + east * px[:, :, 2:]
        + south * py[..., :-2]
        + north * py[..., 2:]
    )
    return core + weight * (source - (diag * core - beside)) / diag


def fix_ends(extended, width, first_plane, total_planes):
    levels = first_plane - width + jnp.arange(extended.shape[0], dtype=jnp.int32)
    levels = levels[:, None, None]
    extended = jnp.where(levels < 0, extended[width][None], extended)
    return jnp.where(
        levels >= total_planes, extended[extended.shape[0] - width - 1][None], extended
    )


def on_device(log_cond, head_slope, modes, obs_cells, obs_var, misfit, base_fields):
    planes, width_x, width_y = log_cond.shape
    local_modes = modes.shape[0]
    first_plane = lax.axis_index("slab") * planes
    total_planes = planes * lax.axis_size("slab")
    cond = jnp.exp(log_cond)
    source = head_slope[None] * cond[None] * modes.astype(jnp.float32)
    weights = sweep_weights(ITERS)
    cond_ext = padded_2(cond, (("slab", 0),), 1)
    coeffs = coefficients(fix_ends(cond_ext, 1, first_plane, total_planes))
    head = jnp.zeros_like(source)
    for weight in weights:
        head_ext = padded_2(head, (("slab", 1),), 1)
        head = relax(head_ext, source, coeffs, weight)
    cells_dev = planes * width_x * width_y
    flat = head.reshape(local_modes, cells_dev)
    picked = jnp.take(flat, obs_cells, axis=1)
    whole = lax.all_gather(picked, "mode", axis=0, tiled=True)
    scaled = whole / obs_var[None, :]
    gram_part = jnp.dot(scaled, whole.T, precision=lax.Precision.HIGHEST)
    rhs_part = jnp.dot(scaled, misfit, precision=lax.Precision.HIGHEST)
    gram, rhs = lax.psum((gram_part, rhs_part), "slab")
    gram = gram + jnp.eye(gram.shape[0], dtype=jnp.float32)
    factor = jnp.linalg.cholesky(gram)
    coef = jax.scipy.linalg.cho_solve((factor, True), rhs)
    block = lax.all_to_all(modes, "mode", split_axis=2, concat_axis=0, tiled=True)
    total_modes, count_planes, cols, rows = block.shape
    layer = block.reshape(total_modes, count_planes * cols * rows).astype(jnp.float32)
    update = jnp.dot(coef.T, layer, precision=lax.Precision.HIGHEST)
    update = update.reshape(coef.shape[1], count_planes, cols, rows)
    return base_fields.astype(jnp.float32) + update


def solution(mesh):
    placed = (
        P("slab", None, None),
        P("slab", None, None),
        P("mode", "slab", None, None),
        P("slab"),
        P("slab"),
        P("slab", None),
        P(None, "slab", "mode", None),
    )
    return jax.shard_map(
        on_device,
        mesh=mesh,
        in_specs=placed,
        out_specs=P(None, "slab", "mode", None),
        check_vma=False,
    )
```

profile of v0, /device:TPU:0, one launch (start us, length us, event | category | flops | bytes accessed | tf_op | source)
XLA Modules:
  0.0 348.2 jit_solution(14503904211151494615)
XLA Ops:
  0.0 1.6 broadcast.132
  1.6 3.7 %collective-permute-start.2 = (f32[32,1,128,128]{3,2,1,0:T(8,128)}, f32[32,1,128,128]{3,2,1,0:T(8,128)}, u32[]{:S(2)}, u32[]{:S(2)}) collective-permute-start(f32[32,1,128,128]{3,2,1,0:T(8,128)} %broadcast.132), channel_id=1, source_target_pairs={{0,1},{1,2},{2,3},{3,4},{4,5},{5,6},{6,7},{7,8},{8,9},{9,10},{10,1... | collective-permute-start | bytes 6291464 | tf_op jit(solution)/shard_map/ppermute | solution.py:22
  5.3 1.3 collective-permute-start.3
  6.5 1.1 exponential_multiply_fusion
  7.6 3.8 %collective-permute-start = (f32[1,128,128]{2,1,0:T(8,128)S(1)}, f32[1,128,128]{2,1,0:T(8,128)S(1)}, u32[]{:S(2)}, u32[]{:S(2)}) collective-permute-start(f32[1,128,128]{2,1,0:T(8,128)S(1)} %get-tuple-element.26), channel_id=1, source_target_pairs={{0,1},{1,2},{2,3},{3,4},{4,5},{5,6},{6,7},{7,8},{8,9},{9,10},{10,1... | collective-permute-start | bytes 196616 | tf_op jit(solution)/shard_map/ppermute | solution.py:22
  11.5 1.3 collective-permute-start.1
  12.8 3.1 collective-permute-done.1
  16.8 1.0 broadcast_in_dim.85
  18.1 9.4 %fusion.31 = f32[32,4,128,128]{3,2,1,0:T(8,128)S(1)} fusion(f32[32,1,128,128]{3,2,1,0:T(8,128)} %collective-permute-done.2, f32[32,1,128,128]{3,2,1,0:T(8,128)} %collective-permute-done.3, f32[32,4,128,128]{3,2,1,0:T(8,128)S(1)} %broadcast_in_dim.85, bf16[32,4,128,128]{3,2,1,0:T(8,128)(2,1)S(1)} %copy-done.1, f32[4,128,128]{2,1,0:T(8,128)S(1)} %get-tuple-element.8, ...), kind=kLoop, calls=%fused_computation.46 | loop fusion | flops 35651584 | bytes 27525120 | tf_op jit(solution)/shard_map/div | solution.py:73
  27.5 3.2 copy-done.4
  30.7 2.5 fusion.66
  33.3 40.9 %collective-permute-start.4 = (f32[32,1,128,128]{3,2,1,0:T(8,128)}, f32[32,1,128,128]{3,2,1,0:T(8,128)}, u32[]{:S(2)}, u32[]{:S(2)}) collective-permute-start(f32[32,1,128,128]{3,2,1,0:T(8,128)} %get-tuple-element.17), channel_id=1, source_target_pairs={{0,1},{1,2},{2,3},{3,4},{4,5},{5,6},{6,7},{7,8},{8,9},{9,10},{10,1... | collective-permute-start | bytes 6291464 | tf_op jit(solution)/shard_map/ppermute | solution.py:22
  74.2 1.3 collective-permute-start.5
  75.5 4.6 %copy.30 = bf16[32,4,128,128]{3,0,1,2:T(8,128)(2,1)} copy(bf16[32,4,128,128]{3,2,1,0:T(8,128)(2,1)S(1)} %copy-done.1) | data formatting | bytes 8388608 | tf_op args[2]
  80.1 5.7 %all-to-all-start = ((bf16[32,4,128,128]{3,0,1,2:T(8,128)(2,1)}), bf16[32,4,128,128]{3,0,1,2:T(8,128)(2,1)}, u32[]{:S(2)}, u32[]{:S(2)}) async-start(bf16[32,4,128,128]{3,0,1,2:T(8,128)(2,1)} %copy.30), calls=%async_computation | async-start | bytes 8388608 | tf_op jit(solution)/shard_map/all_to_all | solution.py:110
  85.8 26.2 %fusion.9 = f32[32,4,128,128]{3,2,1,0:T(8,128)S(1)} fusion(f32[32,4,128,128]{3,2,1,0:T(8,128)} %copy-done.4, f32[32,1,128,128]{3,2,1,0:T(8,128)} %collective-permute-done.5, f32[32,1,128,128]{3,2,1,0:T(8,128)} %collective-permute-done.4, bf16[32,4,128,128]{3,2,1,0:T(8,128)(2,1)} %param.9, f32[4,128,128]{2,1,0:T(8,128)S(1)} %get-tuple-element.8, ...), kind=kLoop, calls=%fused_computation.24 | loop fusion | flops 44040192 | bytes 27262976 | tf_op jit(solution)/shard_map/add | solution.py:73
  112.0 3.2 copy-done.3
  115.2 2.5 fusion.65
  117.8 38.5 %collective-permute-start.6 = (f32[32,1,128,128]{3,2,1,0:T(8,128)}, f32[32,1,128,128]{3,2,1,0:T(8,128)}, u32[]{:S(2)}, u32[]{:S(2)}) collective-permute-start(f32[32,1,128,128]{3,2,1,0:T(8,128)} %get-tuple-element.15), channel_id=1, source_target_pairs={{0,1},{1,2},{2,3},{3,4},{4,5},{5,6},{6,7},{7,8},{8,9},{9,10},{10,1... | collective-permute-start | bytes 6291464 | tf_op jit(solution)/shard_map/ppermute | solution.py:22
  156.3 1.5 collective-permute-start.7
  157.8 6.8 %copy.42 = bf16[32,4,2,64,128]{4,3,1,0,2:T(8,128)(2,1)} copy(bf16[32,4,2,64,128]{4,0,1,3,2:T(8,128)(2,1)} %bitcast.9) | data formatting | bytes 8388608 | tf_op jit(solution)/shard_map/all_to_all | solution.py:110
  164.6 7.3 %reshape.48 = bf16[64,32768]{1,0:T(8,128)(2,1)} reshape(bf16[2,32,4,64,128]{4,3,2,1,0:T(8,128)(2,1)} %bitcast.41) | data formatting | bytes 8388608 | tf_op jit(solution)/shard_map/reshape | solution.py:112
  171.9 5.4 %copy.35 = bf16[8,8,256,128]{3,2,1,0:T(8,128)(2,1)} copy(bf16[8,8,256,128]{3,1,2,0:T(8,128)(2,1)} %bitcast.42) | data formatting | bytes 8388608
  177.4 27.5 %fusion.20 = f32[32,4,128,128]{3,2,1,0:T(8,128)} fusion(f32[32,4,128,128]{3,2,1,0:T(8,128)} %copy-done.3, f32[32,1,128,128]{3,2,1,0:T(8,128)} %collective-permute-done.7, f32[32,1,128,128]{3,2,1,0:T(8,128)} %collective-permute-done.6, bf16[32,4,128,128]{3,2,1,0:T(8,128)(2,1)S(1)} %copy-done.2, f32[4,128,128]{2,1,0:T(8,128)S(1)} %get-tuple-element.8, ...), kind=kLoop, calls=%fused_computation.35 | loop fusion | flops 44040192 | bytes 27262976 | tf_op jit(solution)/shard_map/add | solution.py:73
  204.9 19.9 %copy.27 = f32[32,4,128,128]{0,3,2,1:T(8,128)} copy(f32[32,4,128,128]{3,2,1,0:T(8,128)} %fusion.20) | data formatting | bytes 16777216 | tf_op jit(solution)/shard_map/add | solution.py:73
  224.8 13.3 %gather_fusion = f32[1024,32]{1,0:T(8,128)S(1)} fusion(f32[32,65536]{0,1:T(8,128)} %bitcast.39, s32[1024]{0:T(1024)S(1)} %fusion.62), kind=kCustom, calls=%fused_computation | custom fusion | bytes 266240 | tf_op jit(solution)/shard_map/jit(_take)/gather | solution.py:101
  238.5 5.6 %all_gather.3 = f32[64,1024]{1,0:T(8,128)S(1)} all-gather(f32[32,1024]{1,0:T(8,128)S(1)} %copy.28), channel_id=1, replica_groups=mesh['mode'=2,'slab'=16] {'mode'}, dimensions={0}, use_global_device_ids=true | all-gather | bytes 393216 | tf_op jit(solution)/shard_map/all_gather | solution.py:102
  244.8 82.3 %all-reduce.8 = (f32[64,16]{0,1:T(8,128)S(1)}, f32[64,64]{1,0:T(8,128)S(1)}) all-reduce(f32[64,16]{0,1:T(8,128)S(1)} %fusion.51, f32[64,64]{1,0:T(8,128)S(1)} %fusion.53), channel_id=1, replica_groups=mesh['mode'=2,'slab'=16] {'slab'}, use_global_device_ids=true, to_apply=%region_3.4 | all-reduce | flops 5120 | bytes 40960 | tf_op jit(solution)/shard_map/psum | solution.py:106
  327.2 5.8 %cholesky.17 = f32[64,64]{1,0:T(8,128)S(1)} custom-call(f32[64,64]{1,0:T(8,128)S(1)} %fusion.61), custom_call_target="Cholesky" | custom-call | tf_op jit(solution)/shard_map/jit(cholesky)/cholesky | solution.py:108
  334.4 4.9 %custom-call.10 = f32[1,64,64]{1,2,0:T(8,128)S(1)} custom-call(f32[1,64,64]{2,1,0:T(8,128)S(1)} %fusion.57), custom_call_target="InvertDiagBlocksLowerTriangular" | custom-call | tf_op jit(solution)/shard_map/jit(_cho_solve)/triangular_solve | solution.py:109
  339.6 6.6 %convert_add_fusion = f32[16,4,64,128]{3,0,2,1:T(8,128)S(1)} fusion(f32[64,16,1,1]{0,1,3,2:T(8,128)S(1)} %convolution_bitcast_fusion, bf16[4,64,128,64]{2,1,0,3:T(8,128)(2,1)} %bitcast.40, bf16[16,4,64,128]{3,2,1,0:T(8,128)(2,1)S(1)} %copy-done.5), kind=kOutput, calls=%fused_computation.70 | convolution fusion | flops 403701760 | bytes 7344128 | tf_op jit(solution)/shard_map/dot_general | solution.py:113
  346.3 2.0 copy.33
  (45 shorter events, 3.9 us)
Async XLA Ops:
  0.0 244.5 %copy-start = (f32[1024,16]{0,1:T(8,128)S(1)}, f32[1024,16]{0,1:T(8,128)}, u32[]{:S(2)}) copy-start(f32[1024,16]{0,1:T(8,128)} %param.12) | copy-start | bytes 196612
  1.6 15.3 %collective-permute-start.2 = (f32[32,1,128,128]{3,2,1,0:T(8,128)}, f32[32,1,128,128]{3,2,1,0:T(8,128)}, u32[]{:S(2)}, u32[]{:S(2)}) collective-permute-start(f32[32,1,128,128]{3,2,1,0:T(8,128)} %broadcast.132), channel_id=1, source_target_pairs={{0,1},{1,2},{2,3},{3,4},{4,5},{5,6},{6,7},{7,8},{8,9},{9,10},{10,1... | collective-permute-start | bytes 6291464 | tf_op jit(solution)/shard_map/ppermute | solution.py:22
  5.3 11.6 %collective-permute-start.3 = (f32[32,1,128,128]{3,2,1,0:T(8,128)}, f32[32,1,128,128]{3,2,1,0:T(8,128)}, u32[]{:S(2)}, u32[]{:S(2)}) collective-permute-start(f32[32,1,128,128]{3,2,1,0:T(8,128)} %broadcast.132), channel_id=1, source_target_pairs={{1,0},{2,1},{3,2},{4,3},{5,4},{6,5},{7,6},{8,7},{9,8},{10,9},{11,1... | collective-permute-start | bytes 6291464 | tf_op jit(solution)/shard_map/ppermute | solution.py:24
  7.6 5.2 %collective-permute-start = (f32[1,128,128]{2,1,0:T(8,128)S(1)}, f32[1,128,128]{2,1,0:T(8,128)S(1)}, u32[]{:S(2)}, u32[]{:S(2)}) collective-permute-start(f32[1,128,128]{2,1,0:T(8,128)S(1)} %get-tuple-element.26), channel_id=1, source_target_pairs={{0,1},{1,2},{2,3},{3,4},{4,5},{5,6},{6,7},{7,8},{8,9},{9,10},{10,1... | collective-permute-start | bytes 196616 | tf_op jit(solution)/shard_map/ppermute | solution.py:22
  11.5 4.4 %collective-permute-start.1 = (f32[1,128,128]{2,1,0:T(8,128)S(1)}, f32[1,128,128]{2,1,0:T(8,128)S(1)}, u32[]{:S(2)}, u32[]{:S(2)}) collective-permute-start(f32[1,128,128]{2,1,0:T(8,128)S(1)} %get-tuple-element.27), channel_id=1, source_target_pairs={{1,0},{2,1},{3,2},{4,3},{5,4},{6,5},{7,6},{8,7},{9,8},{10,9},{11,1... | collective-permute-start | bytes 196616 | tf_op jit(solution)/shard_map/ppermute | solution.py:24
  15.9 2.2 copy-start.1
  27.5 3.2 copy-start.4
  33.3 52.5 %collective-permute-start.4 = (f32[32,1,128,128]{3,2,1,0:T(8,128)}, f32[32,1,128,128]{3,2,1,0:T(8,128)}, u32[]{:S(2)}, u32[]{:S(2)}) collective-permute-start(f32[32,1,128,128]{3,2,1,0:T(8,128)} %get-tuple-element.17), channel_id=1, source_target_pairs={{0,1},{1,2},{2,3},{3,4},{4,5},{5,6},{6,7},{7,8},{8,9},{9,10},{10,1... | collective-permute-start | bytes 6291464 | tf_op jit(solution)/shard_map/ppermute | solution.py:22
  74.2 11.6 %collective-permute-start.5 = (f32[32,1,128,128]{3,2,1,0:T(8,128)}, f32[32,1,128,128]{3,2,1,0:T(8,128)}, u32[]{:S(2)}, u32[]{:S(2)}) collective-permute-start(f32[32,1,128,128]{3,2,1,0:T(8,128)} %get-tuple-element.18), channel_id=1, source_target_pairs={{1,0},{2,1},{3,2},{4,3},{5,4},{6,5},{7,6},{8,7},{9,8},{10,9},{11,1... | collective-permute-start | bytes 6291464 | tf_op jit(solution)/shard_map/ppermute | solution.py:24
  80.1 77.7 %all-to-all-start = ((bf16[32,4,128,128]{3,0,1,2:T(8,128)(2,1)}), bf16[32,4,128,128]{3,0,1,2:T(8,128)(2,1)}, u32[]{:S(2)}, u32[]{:S(2)}) async-start(bf16[32,4,128,128]{3,0,1,2:T(8,128)(2,1)} %copy.30), calls=%async_computation | async-start | bytes 8388608 | tf_op jit(solution)/shard_map/all_to_all | solution.py:110
  112.0 3.2 copy-start.3
  115.2 42.5 %copy-start.6 = (s32[1024]{0:T(1024)S(1)}, s32[1024]{0:T(1024)}, u32[]{:S(2)}) copy-start(s32[1024]{0:T(1024)} %param.10) | copy-start | bytes 12292
  117.8 59.6 %collective-permute-start.6 = (f32[32,1,128,128]{3,2,1,0:T(8,128)}, f32[32,1,128,128]{3,2,1,0:T(8,128)}, u32[]{:S(2)}, u32[]{:S(2)}) collective-permute-start(f32[32,1,128,128]{3,2,1,0:T(8,128)} %get-tuple-element.15), channel_id=1, source_target_pairs={{0,1},{1,2},{2,3},{3,4},{4,5},{5,6},{6,7},{7,8},{8,9},{9,10},{10,1... | collective-permute-start | bytes 6291464 | tf_op jit(solution)/shard_map/ppermute | solution.py:22
  156.3 21.1 %collective-permute-start.7 = (f32[32,1,128,128]{3,2,1,0:T(8,128)}, f32[32,1,128,128]{3,2,1,0:T(8,128)}, u32[]{:S(2)}, u32[]{:S(2)}) collective-permute-start(f32[32,1,128,128]{3,2,1,0:T(8,128)} %get-tuple-element.16), channel_id=1, source_target_pairs={{1,0},{2,1},{3,2},{4,3},{5,4},{6,5},{7,6},{8,7},{9,8},{10,9},{11,1... | collective-permute-start | bytes 6291464 | tf_op jit(solution)/shard_map/ppermute | solution.py:24
  171.9 5.4 %copy-start.2 = (bf16[32,4,128,128]{3,2,1,0:T(8,128)(2,1)S(1)}, bf16[32,4,128,128]{3,2,1,0:T(8,128)(2,1)}, u32[]{:S(2)}) copy-start(bf16[32,4,128,128]{3,2,1,0:T(8,128)(2,1)} %param.9) | copy-start | bytes 12582916
  204.9 39.3 %copy-start.7 = (f32[1024]{0:T(1024)S(1)}, f32[1024]{0:T(1024)}, u32[]{:S(2)}) copy-start(f32[1024]{0:T(1024)} %param.11) | copy-start | bytes 12292
  204.9 134.7 %copy-start.5 = (bf16[16,4,64,128]{3,2,1,0:T(8,128)(2,1)S(1)}, bf16[16,4,64,128]{3,2,1,0:T(8,128)(2,1)}, u32[]{:S(2)}) copy-start(bf16[16,4,64,128]{3,2,1,0:T(8,128)(2,1)} %param.13) | copy-start | bytes 3145732
where the time goes:
time: 349 us; the launch traced here: 348 us
  starting transfers between devices  98 us (28%)
  blocking collectives  87.9 us (25%)
  other arithmetic  77.2 us (22%)
  local copies, waits for them, and re-layouts  74.2 us (21%)
  matrix products  7.56 us (2%)
    ppermute x4, starting transfers between devices, padded_2(): lax.ppermute(tail, axis, [(i, (i + 1) % count) for i in range(ends)])  87 us
    psum x1, blocking collectives, on_device(): gram, rhs = lax.psum((gram_part, rhs_part), 'slab')  82.3 us
    add x2, other arithmetic, relax(): return core + weight * (source - (diag * core - beside)) / diag  53.7 us
    add x1, local copies, waits for them, and re-layouts, relax(): return core + weight * (source - (diag * core - beside)) / diag  19.9 us
    unnamed x18, local copies, waits for them, and re-layouts  16.7 us
    gather x1, local copies, waits for them, and re-layouts, on_device(): picked = jnp.take(flat, obs_cells, axis=1)  13.3 us
    div x1, other arithmetic, relax(): return core + weight * (source - (diag * core - beside)) / diag  9.38 us
    reshape x1, local copies, waits for them, and re-layouts, on_device(): block.reshape(total_modes, count_planes * cols * rows).astype(jnp.float32)  7.3 us
  transfers between devices with their start and end apart: 9, of which 1 were waited for; matrix products, arithmetic and copies ran while one was open for 16% of the time, Pallas kernels for 0%

commit v1 on v0

v1 whole, which is shorter than its diff:
```python
import functools
import math

import jax
import jax.numpy as jnp
from jax import lax
from jax.experimental import pallas as pl
from jax.experimental.pallas import tpu as pltpu
from jax.sharding import PartitionSpec as P

ITERS = 3
STORAGE = 0.05
REACH = ITERS - 1
MIB = 1 << 20


def sweep_weights(count):
    order = []
    low, high = (0, count - 1)
    while low <= high:
        order.append(low)
        if high != low:
            order.append(high)
        low += 1
        high -= 1
    return [1.0 / (1.15 + 0.85 * math.cos((2 * i + 1) * math.pi / (2 * count))) for i in order]


W0, W1, W2 = sweep_weights(ITERS)
SCALE_B = W0 * W1
SCALE_A = (1.0 - W1) * W0 + W1
SELF_2 = SCALE_A / SCALE_B
SELF_3 = (1.0 - W2) / W2
SOURCE_3 = 1.0 / SCALE_B


def stencil_kernel(
    planes, width, modes_count, group, edge_ref, cells_ref, cells_b_ref, cells_a_ref,
    log_ref, slope_ref, modes_ref, own_ref, below_ref, above_ref,
    coef, gain, cond, t_ref, u_ref, r_ref,
):
    step = pl.program_id(0)
    lanes = log_ref.shape[-1]
    pad = 8
    tiles = width // 8
    stride = (planes + 2 * REACH) * width + pad
    n_ext = planes + 2 * REACH + 2

    @pl.when(step == 0)
    def _():
        cond[...] = jnp.ones_like(cond)
        for z in range(n_ext):
            cond[pl.ds(pad + z * width, width), :] = jnp.exp(log_ref[z])

        @pl.when(edge_ref[0] == 1)
        def _():
            cond[pl.ds(pad + 2 * width, width), :] = cond[pl.ds(pad + 3 * width, width), :]

        @pl.when(edge_ref[1] == 1)
        def _():
            cond[pl.ds(pad + (planes + 3) * width, width), :] = cond[
                pl.ds(pad + (planes + 2) * width, width), :
            ]

        t_ref[...] = jnp.zeros_like(t_ref)
        u_ref[...] = jnp.zeros_like(u_ref)
        rows = lax.broadcasted_iota(jnp.int32, (8, lanes), 0)
        cols = lax.broadcasted_iota(jnp.int32, (8, lanes), 1)
        first = edge_ref[0] == 1
        last = edge_ref[1] == 1
        for z in range(planes + 2 * REACH):
            def body(i, carry, z=z):
                at = pad + (z + 1) * width + i * 8
                c = cond[pl.ds(at, 8), :]

                def harmonic(other):
                    return 2.0 * c * other / (c + other)

                x = rows + i * 8
                lower = harmonic(cond[pl.ds(at - width, 8), :])
                upper = harmonic(cond[pl.ds(at + width, 8), :])
                west = harmonic(jnp.where(x == 0, c, cond[pl.ds(at - 1, 8), :]))
                east = harmonic(jnp.where(x == width - 1, c, cond[pl.ds(at + 1, 8), :]))
                south = harmonic(jnp.where(cols == 0, c, pltpu.roll(c, 1, axis=1)))
                north = harmonic(jnp.where(cols == lanes - 1, c, pltpu.roll(c, lanes - 1, axis=1)))
                inverse = 1.0 / (STORAGE + lower + upper + west + east + south + north)
                zero = jnp.zeros_like(c)
                if z < REACH:
                    upper = jnp.where(first, zero, upper)
                if z == REACH:
                    lower = jnp.where(first, zero, lower)
                if z == REACH + planes - 1:
                    upper = jnp.where(last, zero, upper)
                if z >= REACH + planes:
                    lower = jnp.where(last, zero, lower)
                here = pl.ds(i * 8, 8)
                coef[z, 0, here, :] = lower * inverse
                coef[z, 1, here, :] = upper * inverse
                coef[z, 2, here, :] = jnp.where(x == 0, zero, west * inverse)
                coef[z, 3, here, :] = jnp.where(x == width - 1, zero, east * inverse)
                coef[z, 4, here, :] = jnp.where(cols == 0, zero, south * inverse)
                coef[z, 5, here, :] = jnp.where(cols == lanes - 1, zero, north * inverse)
                if REACH <= z < REACH + planes:
                    gain[z - REACH, here, :] = (
                        (W2 * SCALE_B) * slope_ref[z - REACH, here, :] * c * inverse
                    )
                return carry

            lax.fori_loop(0, tiles, body, 0)
        for k in range(modes_count):
            r_ref[pl.ds(k * stride + stride - pad, pad), :] = jnp.zeros((pad, lanes), jnp.float32)

    for z in range(planes):
        def convert(i, carry, z=z):
            here = pl.ds(i * 16, 16)
            g = gain[z, here, :]
            for m in range(group):
                t_ref[m, pl.ds(pad + z * width + i * 16, 16), :] = g * modes_ref[
                    m, z, here, :
                ].astype(jnp.float32)
            return carry

        lax.fori_loop(0, width // 16, convert, 0)

    def beside(ref, m, at, c, terms):
        total = None
        centre = ref[m, pl.ds(at, 8), :]
        for name in terms:
            if name == 0:
                v = ref[m, pl.ds(at - width, 8), :]
            elif name == 1:
                v = ref[m, pl.ds(at + width, 8), :]
            elif name == 2:
                v = ref[m, pl.ds(at - 1, 8), :]
            elif name == 3:
                v = ref[m, pl.ds(at + 1, 8), :]
            elif name == 4:
                v = pltpu.roll(centre, 1, axis=1)
            else:
                v = pltpu.roll(centre, lanes - 1, axis=1)
            v = c[name] * v
            total = v if total is None else total + v
        return centre, total

    for z in range(-1, planes + 1):
        if z == -1:
            terms = (1,)
        elif z == planes:
            terms = (0,)
        else:
            terms = (2, 3, 4, 5) + ((0,) if z > 0 else ()) + ((1,) if z < planes - 1 else ())

        def second(i, carry, z=z, terms=terms):
            c = {n: coef[z + REACH, n, pl.ds(i * 8, 8), :] for n in terms}
            at = pad + z * width + i * 8
            put = pl.ds(pad + (z + 1) * width + i * 8, 8)
            for m in range(group):
                if 0 <= z < planes:
                    centre, total = beside(t_ref, m, at, c, terms)
                    total = total + SELF_2 * centre
                elif z == -1:
                    total = c[1] * t_ref[m, pl.ds(at + width, 8), :]
                else:
                    total = c[0] * t_ref[m, pl.ds(at - width, 8), :]
                u_ref[m, put, :] = total
            return carry

        lax.fori_loop(0, tiles, second, 0)

    for z in range(-2, planes + 2):
        if z == -2:
            terms = (1,)
        elif z == planes + 1:
            terms = (0,)
        else:
            terms = (2, 3, 4, 5) + ((0,) if z > -1 else ()) + ((1,) if z < planes else ())

        def third(i, carry, z=z, terms=terms):
            c = {n: coef[z + REACH, n, pl.ds(i * 8, 8), :] for n in terms}
            at = pad + (z + 1) * width + i * 8
            for m in range(group):
                if z == -2:
                    total = c[1] * u_ref[m, pl.ds(at + width, 8), :]
                elif z == planes + 1:
                    total = c[0] * u_ref[m, pl.ds(at - width, 8), :]
                else:
                    centre, total = beside(u_ref, m, at, c, terms)
                    total = total + SELF_3 * centre
                    if 0 <= z < planes:
                        total = total + SOURCE_3 * t_ref[m, pl.ds(pad + z * width + i * 8, 8), :]
                put = pl.multiple_of(
                    (step * group + m) * stride + (z + REACH) * width + i * 8, 8
                )
                r_ref[pl.ds(put, 8), :] = total
            return carry

        lax.fori_loop(0, tiles, third, 0)

    @pl.when(step == pl.num_programs(0) - 1)
    def _():
        cols = lax.broadcasted_iota(jnp.int32, (modes_count, lanes), 1)
        count = cells_ref.shape[0]
        zero_row = stride - pad
        shift = lanes.bit_length() - 1

        def pick(cells, out, low, high, offset):
            def block(b, carry):
                def one(i, acc):
                    cell = cells[b * lanes + i]
                    row = cell >> shift
                    lane = cell & (lanes - 1)
                    if low is not None:
                        inside = jnp.logical_and(row >= low, row < high)
                        row = jnp.where(inside, row + offset, zero_row)
                    else:
                        row = row + offset
                    v = r_ref[pl.ds(row, modes_count, stride=stride), :]
                    v = pltpu.roll(v, (i - lane) & (lanes - 1), axis=1)
                    return jnp.where(cols == i, v, acc)

                acc = lax.fori_loop(
                    0, lanes, one, jnp.zeros((modes_count, lanes), jnp.float32), unroll=8
                )
                out[:, pl.ds(pl.multiple_of(b * lanes, lanes), lanes)] = acc
                return carry

            lax.fori_loop(0, count // lanes, block, 0)

        pick(cells_ref, own_ref, None, None, REACH * width)
        pick(
            cells_b_ref, below_ref, (planes - REACH) * width, planes * width,
            (REACH - planes) * width,
        )
        pick(cells_a_ref, above_ref, 0, REACH * width, (REACH + planes) * width)


def stencil(edges, cells, cells_b, cells_a, log_ext, slope, modes):
    modes_count, planes, width, lanes = modes.shape
    count = cells.shape[0]
    group = 4
    n_ext = planes + 2 * REACH + 2
    stride = (planes + 2 * REACH) * width + 8
    smem = pl.BlockSpec(memory_space=pltpu.SMEM)
    vmem = pl.BlockSpec(memory_space=pltpu.VMEM)
    shape = jax.ShapeDtypeStruct((modes_count, count), jnp.float32)
    return pl.pallas_call(
        functools.partial(stencil_kernel, planes, width, modes_count, group),
        grid=(modes_count // group,),
        out_shape=(shape, shape, shape),
        in_specs=[smem] * 4
        + [vmem, vmem, pl.BlockSpec((group, planes, width, lanes), lambda s: (s, 0, 0, 0))],
        out_specs=(pl.BlockSpec((modes_count, count), lambda s: (0, 0)),) * 3,
        scratch_shapes=[
            pltpu.VMEM((planes + 2 * REACH, 6, width, lanes), jnp.float32),
            pltpu.VMEM((planes, width, lanes), jnp.float32),
            pltpu.VMEM((n_ext * width + 16, lanes), jnp.float32),
            pltpu.VMEM((group, planes * width + 16, lanes), jnp.float32),
            pltpu.VMEM((group, (planes + 2) * width + 16, lanes), jnp.float32),
            pltpu.VMEM((modes_count * stride, lanes), jnp.float32),
        ],
        compiler_params=pltpu.CompilerParams(
            dimension_semantics=("arbitrary",), vmem_limit_bytes=40 * MIB
        ),
        cost_estimate=pl.CostEstimate(
            flops=40 * modes.size, bytes_accessed=4 * modes.size, transcendentals=0
        ),
        name="stencil",
    )(edges, cells, cells_b, cells_a, log_ext, slope, modes)


def solve_kernel(gram_ref, rhs_ref, out_ref, work):
    n = gram_ref.shape[0]
    f = rhs_ref.shape[1]
    work[...] = jnp.zeros_like(work)
    rows = lax.broadcasted_iota(jnp.int32, (n, n), 0)
    cols = lax.broadcasted_iota(jnp.int32, (n, n), 1)
    work[:, :n] = gram_ref[...] + jnp.where(rows == cols, 1.0, 0.0)
    work[:, n : n + f] = rhs_ref[...]
    matrix = work[...]
    tall = lax.broadcasted_iota(jnp.int32, matrix.shape, 0)
    for j in range(n):
        row = matrix[j : j + 1, :]
        row = row / row[:, j : j + 1]
        column = matrix[:, j : j + 1]
        matrix = jnp.where(tall == j, row, matrix - column * row)
    work[...] = matrix
    out_ref[...] = work[:, n : n + f]


def solve(gram, rhs):
    n, f = rhs.shape
    return pl.pallas_call(
        solve_kernel,
        out_shape=jax.ShapeDtypeStruct((n, f), jnp.float32),
        scratch_shapes=[pltpu.VMEM((n, 128 * pl.cdiv(n + f, 128)), jnp.float32)],
        name="solve",
    )(gram, rhs)


def update_kernel(place_ref, coef_ref, own_ref, others_ref, base_ref, out_ref, big):
    fields, deep, rows, lanes = out_ref.shape
    total = coef_ref.shape[0]
    mine = own_ref.shape[0]

    @pl.when(jnp.logical_and(pl.program_id(0) == 0, pl.program_id(1) == 0))
    def _():
        coef = coef_ref[...]
        high = coef.astype(jnp.bfloat16)
        low = (coef - high.astype(jnp.float32)).astype(jnp.bfloat16)
        tall, wide = fields * rows, total * rows
        r0 = lax.broadcasted_iota(jnp.int32, (tall, fields), 0)
        f0 = lax.broadcasted_iota(jnp.int32, (tall, fields), 1)
        spread_f = jnp.where(r0 // rows == f0, 1.0, 0.0).astype(jnp.bfloat16)
        k0 = lax.broadcasted_iota(jnp.int32, (total, wide), 0)
        c0 = lax.broadcasted_iota(jnp.int32, (total, wide), 1)
        spread_k = jnp.where(c0 // rows == k0, 1.0, 0.0).astype(jnp.bfloat16)
        r1 = lax.broadcasted_iota(jnp.int32, (tall, wide), 0)
        c1 = lax.broadcasted_iota(jnp.int32, (tall, wide), 1)
        same = r1 % rows == c1 % rows
        for p, part in enumerate((high, low)):
            a = lax.dot_general(
                spread_f, part, (((1,), (1,)), ((), ())), preferred_element_type=jnp.float32
            ).astype(jnp.bfloat16)
            b = jnp.dot(a, spread_k, preferred_element_type=jnp.float32)
            big[p * tall : (p + 1) * tall, :] = jnp.where(same, b, 0.0).astype(jnp.bfloat16)

    tall = fields * rows
    left = mine * rows

    def side(ref):
        count = ref.shape[0]
        return jnp.concatenate(
            [ref[:, d].reshape(count * rows, lanes) for d in range(deep)], axis=1
        )

    both = jnp.dot(big[:, :left], side(own_ref), preferred_element_type=jnp.float32)
    both = both + jnp.dot(big[:, left:], side(others_ref), preferred_element_type=jnp.float32)
    both = both[:tall] + both[tall:]
    for d in range(deep):
        part = both[:, d * lanes : (d + 1) * lanes].reshape(fields, rows, lanes)
        out_ref[:, d] = base_ref[:, d].astype(jnp.float32) + part


def update(place, coef, modes, others, base):
    fields, planes, width, lanes = base.shape
    mine = modes.shape[0]
    rest = others.shape[0]
    rows = 16
    deep = 2
    steps = width // rows

    def fixed(count):
        return pl.BlockSpec((count, deep, rows, lanes), lambda z, x, place: (0, z, x, 0))

    return pl.pallas_call(
        update_kernel,
        grid_spec=pltpu.PrefetchScalarGridSpec(
            num_scalar_prefetch=1,
            grid=(planes // deep, steps),
            in_specs=[
                pl.BlockSpec(coef.shape, lambda z, x, place: (0, 0)),
                pl.BlockSpec(
                    (mine, deep, rows, lanes),
                    lambda z, x, place: (0, z, place[0] * steps + x, 0),
                ),
                fixed(rest),
                fixed(fields),
            ],
            out_specs=fixed(fields),
            scratch_shapes=[
                pltpu.VMEM((2 * fields * rows, (mine + rest) * rows), jnp.bfloat16)
            ],
        ),
        out_shape=jax.ShapeDtypeStruct(base.shape, jnp.float32),
        compiler_params=pltpu.CompilerParams(
            dimension_semantics=("arbitrary", "arbitrary"), vmem_limit_bytes=32 * MIB
        ),
        name="update",
    )(place, coef, modes, others, base)


def on_device(log_cond, head_slope, modes, obs_cells, obs_var, misfit, base_fields):
    planes, width, lanes = log_cond.shape
    n_mode = lax.axis_size("mode")
    n_slab = lax.axis_size("slab")
    me = lax.axis_index("mode")
    level = lax.axis_index("slab")
    part = width // n_mode

    received = []
    for d in range(1, n_mode):
        to = (me + d) % n_mode
        piece = lax.dynamic_slice_in_dim(modes, to * part, part, axis=2)
        received.append(
            lax.ppermute(piece, "mode", [(i, (i + d) % n_mode) for i in range(n_mode)])
        )
    others = received[0] if n_mode == 2 else jnp.concatenate(received, axis=0)

    up = [(i, i + 1) for i in range(n_slab - 1)]
    down = [(i + 1, i) for i in range(n_slab - 1)]
    halo = REACH + 1
    cells_f = obs_cells.astype(jnp.float32).reshape(-1, lanes)

    def message(planes_out):
        return jnp.concatenate([planes_out.reshape(-1, lanes), cells_f], axis=0)

    from_below = lax.ppermute(message(log_cond[-halo:]), "slab", up)
    from_above = lax.ppermute(message(log_cond[:halo]), "slab", down)
    log_ext = jnp.concatenate(
        [
            from_below[: halo * width].reshape(halo, width, lanes),
            log_cond,
            from_above[: halo * width].reshape(halo, width, lanes),
        ],
        axis=0,
    )
    cells_b = from_below[halo * width :].reshape(-1).astype(jnp.int32)
    cells_a = from_above[halo * width :].reshape(-1).astype(jnp.int32)
    edges = jnp.stack([level == 0, level == n_slab - 1]).astype(jnp.int32)
    own, below, above = stencil(edges, obs_cells, cells_b, cells_a, log_ext, head_slope, modes)
    picked = own + lax.ppermute(above, "slab", up) + lax.ppermute(below, "slab", down)
    return picked, others, me


def finish(own, others, me, modes, obs_var, misfit, base_fields):
    n_mode = lax.axis_size("mode")
    mine = modes.shape[0]
    split = own.shape[1] // n_mode
    whole = lax.all_to_all(own, "mode", split_axis=1, concat_axis=0, tiled=True)
    var = lax.dynamic_slice_in_dim(obs_var, me * split, split, axis=0)
    miss = lax.dynamic_slice_in_dim(misfit, me * split, split, axis=0)
    scaled = whole / var[None, :]
    right = jnp.concatenate([whole.T, miss], axis=1)
    both = jnp.dot(scaled, right, precision=lax.Precision.HIGHEST)
    both = lax.psum(both, ("mode", "slab"))
    total = mine * n_mode
    coef = solve(both[:, :total], both[:, total:])
    order = (me - jnp.arange(n_mode)) % n_mode
    coef = coef.reshape(n_mode, mine, -1)[order].reshape(total, -1)
    return update(me.astype(jnp.int32).reshape(1), coef, modes, others, base_fields)


def both_phases(log_cond, head_slope, modes, obs_cells, obs_var, misfit, base_fields):
    picked, others, me = on_device(
        log_cond, head_slope, modes, obs_cells, obs_var, misfit, base_fields
    )
    return finish(picked, others, me, modes, obs_var, misfit, base_fields)


def solution(mesh):
    placed = (
        P("slab", None, None),
        P("slab", None, None),
        P("mode", "slab", None, None),
        P("slab"),
        P("slab"),
        P("slab", None),
        P(None, "slab", "mode", None),
    )
    return jax.shard_map(
        both_phases,
        mesh=mesh,
        in_specs=placed,
        out_specs=P(None, "slab", "mode", None),
        check_vma=False,
    )
```

time: 349 us -> 258 us (0.74)
  Pallas kernels: 0 us -> 176 us
  starting transfers between devices: 98 us -> 17.5 us
  other arithmetic: 77.2 us -> 1.19 us
  local copies, waits for them, and re-layouts: 74.2 us -> 10.4 us
  blocking collectives: 87.9 us -> 42.2 us
  matrix products: 7.56 us -> 0.29 us
  waiting for transfers between devices: 3.08 us -> 9.92 us
    pallas_call x0 -> x3, Pallas kernels: none -> 176 us  [the longest x1 163 us: stencil(): pl.pallas_call(functools.partial(stencil_kernel, planes, width, modes_cou...]
    ppermute x8 -> x5, starting transfers between devices: 92.3 us -> 14.2 us  [the longest x1 7.17 us: on_device(): lax.ppermute(above, 'slab', up)]
    add x3 -> x1, other arithmetic: 53.7 us -> 0.99 us  [on_device(): own + lax.ppermute(above, 'slab', up) + lax.ppermute(below, 'slab', down)]
    psum x1, blocking collectives: 82.3 us -> 42.2 us  [finish(): both = lax.psum(both, ('mode', 'slab'))]
    add x3 -> x0, local copies, waits for them, and re-layouts: 21.9 us -> none  [the longest x1 19.9 us: relax(): return core + weight * (source - (diag * core - beside)) / diag]
    unnamed x18, local copies, waits for them, and re-layouts: 16.7 us -> 4.39 us
    another operation x5 -> x0, other arithmetic: 12.1 us -> none  [the longest x3 6.52 us: on_device(): factor = jnp.linalg.cholesky(gram)]
    gather x1, local copies, waits for them, and re-layouts: 13.3 us -> 1.3 us  [finish(): coef = coef.reshape(n_mode, mine, -1)[order].reshape(total, -1)]
  transfers between devices with their start and end apart: 9 -> 6, of which waited for: 1 -> 3; matrix products, arithmetic and copies ran while one was open for 16% -> 2% of each run, Pallas kernels for 0% -> 66%
where the time goes in v1:
time: 258 us
  Pallas kernels  176 us (68%)
  blocking collectives  42.2 us (16%)
  starting transfers between devices  17.5 us (7%)
  local copies, waits for them, and re-layouts  10.4 us (4%)
  waiting for transfers between devices  9.92 us (4%)
    pallas_call x1, Pallas kernels, stencil(): pl.pallas_call(functools.partial(stencil_kernel, planes, width, modes_cou...  163 us
    psum x1, blocking collectives, finish(): both = lax.psum(both, ('mode', 'slab'))  42.2 us
    ppermute x1, starting transfers between devices, on_device(): lax.ppermute(above, 'slab', up)  7.17 us
    pallas_call x1, Pallas kernels, solve(): pl.pallas_call(solve_kernel, out_shape=jax.ShapeDtypeStruct((n, f), jnp.f...  6.95 us
    pallas_call x1, Pallas kernels, update(): pl.pallas_call(update_kernel, grid_spec=pltpu.PrefetchScalarGridSpec(num_...  6.25 us
  transfers between devices with their start and end apart: 6, of which 3 were waited for; matrix products, arithmetic and copies ran while one was open for 2% of the time, Pallas kernels for 66%

profile of v1, /device:TPU:0, one launch (start us, length us, event | category | flops | bytes accessed | tf_op | source)
XLA Modules:
  0.0 257.6 jit_solution(6974348702681063165)
XLA Ops:
  0.0 3.2 %constant_dynamic-slice_fusion = bf16[32,4,64,128]{3,2,1,0:T(8,128)(2,1)} fusion(bf16[32,4,128,128]{3,2,1,0:T(8,128)(2,1)} %own_ref.1, s32[]{:T(128)S(6)} %select_n.41), kind=kLoop, calls=%fused_computation.24 | loop fusion | bytes 4194308 | tf_op jit(solution)/shard_map/dynamic_slice | solution.py:393
  3.3 2.9 %collective-permute-start.4 = (bf16[32,4,64,128]{3,2,1,0:T(8,128)(2,1)}, bf16[32,4,64,128]{3,2,1,0:T(8,128)(2,1)S(1)}, u32[]{:S(2)}, u32[]{:S(2)}) collective-permute-start(bf16[32,4,64,128]{3,2,1,0:T(8,128)(2,1)} %constant_dynamic-slice_fusion), channel_id=1, source_target_pairs={{0,16},{16,0},{1,17},{17,1},{2,18},{18,2},{3,19},{19,3},{4,20},{20... | collective-permute-start | bytes 6291464 | tf_op jit(solution)/shard_map/ppermute | solution.py:395
  6.3 1.5 collective-permute-start
  7.8 1.3 collective-permute-start.1
  9.1 0.1 add_convert_fusion.edge_ref
  9.2 0.0 collective-permute-done
  9.2 3.5 %collective-permute-done.1 = f32[392,128]{1,0:T(8,128)S(1)} collective-permute-done((f32[392,128]{1,0:T(8,128)S(1)}, f32[392,128]{1,0:T(8,128)S(1)}, u32[]{:S(2)}, u32[]{:S(2)}) %collective-permute-start.1) | collective-permute-done | bytes 200736 | tf_op jit(solution)/shard_map/ppermute | solution.py:408
  12.8 0.0 copy-done.4
  12.8 0.0 copy-start.1
  12.8 2.2 copy-done.1
  15.0 162.6 %stencil.1 = (f32[32,1024]{1,0:T(8,128)S(1)}, f32[32,1024]{1,0:T(8,128)S(1)}, f32[32,1024]{1,0:T(8,128)}) custom-call(s32[2]{0:T(128)S(1)} %add_convert_fusion.edge_ref, s32[1024]{0:T(1024)S(1)} %copy-done.5, s32[1024]{0:T(1024)S(1)} %fusion.5.cells_b_ref, s32[1024]{0:T(1024)S(1)} %fusion.4.cells_a_ref, f32[10,128,128]{2,1,0:T(8,128)S(1)} %pad_maximum_fusion.log_ref, ...), custom_call_target="tpu_custom_call" | custom-call | flops 83886080 | bytes 8388608 | tf_op jit(solution)/shard_map/stencil/pallas_call | solution.py:246
  177.6 7.2 %collective-permute-start.2 = (f32[32,1024]{1,0:T(8,128)}, f32[32,1024]{1,0:T(8,128)}, u32[]{:S(2)}, u32[]{:S(2)}) collective-permute-start(f32[32,1024]{1,0:T(8,128)} %get-tuple-element.9), channel_id=1, source_target_pairs={{0,1},{1,2},{2,3},{3,4},{4,5},{5,6},{6,7},{7,8},{8,9},{9,10},{10,1... | collective-permute-start | bytes 393224 | tf_op jit(solution)/shard_map/ppermute | solution.py:421
  184.7 1.3 collective-permute-start.3
  186.0 0.0 copy-done.8
  186.0 0.1 dynamic_slice.9
  186.1 0.0 collective-permute-done.2
  186.1 2.0 collective-permute-done.3
  188.1 1.0 add_add_fusion
  189.1 0.7 copy.11
  189.8 3.4 %all-to-all-start = ((f32[32,2,512]{2,0,1:T(8,128)}), f32[32,2,512]{2,0,1:T(8,128)S(1)}, u32[]{:S(2)}, u32[]{:S(2)}) async-start(f32[32,2,512]{2,0,1:T(8,128)} %bitcast.27), calls=%async_computation | async-start | bytes 262144 | tf_op jit(solution)/shard_map/all_to_all | solution.py:429
  193.2 4.4 %all-to-all-done = f32[32,2,512]{2,0,1:T(8,128)S(1)} async-done(((f32[32,2,512]{2,0,1:T(8,128)}), f32[32,2,512]{2,0,1:T(8,128)S(1)}, u32[]{:S(2)}, u32[]{:S(2)}) %all-to-all-start) | async-done | bytes 131104 | tf_op jit(solution)/shard_map/all_to_all | solution.py:429
  197.6 0.3 fusion
  197.9 42.2 %psum.7 = f32[64,80]{1,0:T(8,128)S(1)} all-reduce(f32[64,80]{1,0:T(8,128)S(1)} %fusion), channel_id=1, replica_groups=mesh['mode'=2,'slab'=16] {'mode','slab'}, use_global_device_ids=true, to_apply=%region_0.1 | all-reduce | flops 5120 | bytes 40960 | tf_op jit(solution)/shard_map/psum | solution.py:435
  240.2 0.7 slice.39.rhs_ref
  240.9 0.0 copy-done.7
  240.9 7.0 %solve.1 = f32[64,16]{1,0:T(8,128)} custom-call(f32[64,64]{1,0:T(8,128)} %bitcast.36, f32[64,16]{1,0:T(8,128)} %slice.39.rhs_ref), custom_call_target="tpu_custom_call" | custom-call | tf_op jit(solution)/shard_map/solve/pallas_call | solution.py:292
  247.8 1.3 gather_fusion
  249.1 0.0 collective-permute-done.4.others_ref
  249.2 0.0 copy-done.3
  249.2 0.0 copy-start.2
  249.2 2.2 copy-done.2
  251.4 6.2 %update.1 = f32[16,4,64,128]{3,2,1,0:T(8,128)} custom-call(s32[1]{0:T(128)} %bitcast.place_ref, f32[64,16]{1,0:T(8,128)S(1)} %bitcast.29, bf16[32,4,128,128]{3,2,1,0:T(8,128)(2,1)S(1)} %copy-done.2, bf16[32,4,64,128]{3,2,1,0:T(8,128)(2,1)S(1)} %collective-permute-done.4.others_ref, bf16[16,4,64,128]{3,2,1,0:T(8,128)(2,1)S(1)} %copy-done.3), custom_call_target="tpu_custom_call" | custom-call | tf_op jit(solution)/shard_map/update/pallas_call | solution.py:355
  (22 shorter events, 0.2 us)
Async XLA Ops:
  0.0 186.1 %copy-start = (f32[1024,16]{0,1:T(8,128)S(1)}, f32[1024,16]{0,1:T(8,128)}, u32[]{:S(2)}) copy-start(f32[1024,16]{0,1:T(8,128)} %param.12) | copy-start | bytes 196612
  0.0 6.2 %copy-start.6 = (f32[4,128,128]{2,1,0:T(8,128)S(1)}, f32[4,128,128]{2,1,0:T(8,128)}, u32[]{:S(2)}) copy-start(f32[4,128,128]{2,1,0:T(8,128)} %param.7) | copy-start | bytes 786436
  0.0 6.2 %copy-start.5 = (s32[1024]{0:T(1024)S(1)}, s32[1024]{0:T(1024)}, u32[]{:S(2)}) copy-start(s32[1024]{0:T(1024)} %cells_ref.1) | copy-start | bytes 12292
  3.3 9.5 %copy-start.4 = (f32[4,128,128]{2,1,0:T(8,128)S(1)}, f32[4,128,128]{2,1,0:T(8,128)}, u32[]{:S(2)}) copy-start(f32[4,128,128]{2,1,0:T(8,128)} %slope_ref.1) | copy-start | bytes 786436
  3.3 245.9 %collective-permute-start.4 = (bf16[32,4,64,128]{3,2,1,0:T(8,128)(2,1)}, bf16[32,4,64,128]{3,2,1,0:T(8,128)(2,1)S(1)}, u32[]{:S(2)}, u32[]{:S(2)}) collective-permute-start(bf16[32,4,64,128]{3,2,1,0:T(8,128)(2,1)} %constant_dynamic-slice_fusion), channel_id=1, source_target_pairs={{0,16},{16,0},{1,17},{17,1},{2,18},{18,2},{3,19},{19,3},{4,20},{20... | collective-permute-start | bytes 6291464 | tf_op jit(solution)/shard_map/ppermute | solution.py:395
  6.3 2.9 %collective-permute-start = (f32[392,128]{1,0:T(8,128)S(1)}, f32[392,128]{1,0:T(8,128)S(1)}, u32[]{:S(2)}, u32[]{:S(2)}) collective-permute-start(f32[392,128]{1,0:T(8,128)S(1)} %get-tuple-element.14), channel_id=1, source_target_pairs={{0,1},{1,2},{2,3},{3,4},{4,5},{5,6},{6,7},{7,8},{8,9},{9,10},{10,1... | collective-permute-start | bytes 602120 | tf_op jit(solution)/shard_map/ppermute | solution.py:407
  7.8 4.9 %collective-permute-start.1 = (f32[392,128]{1,0:T(8,128)S(1)}, f32[392,128]{1,0:T(8,128)S(1)}, u32[]{:S(2)}, u32[]{:S(2)}) collective-permute-start(f32[392,128]{1,0:T(8,128)S(1)} %get-tuple-element.13), channel_id=1, source_target_pairs={{1,0},{2,1},{3,2},{4,3},{5,4},{6,5},{7,6},{8,7},{9,8},{10,9},{11,1... | collective-permute-start | bytes 602120 | tf_op jit(solution)/shard_map/ppermute | solution.py:408
  12.8 2.2 copy-start.1
  15.0 171.0 %copy-start.8 = (f32[1024]{0:T(1024)S(1)}, f32[1024]{0:T(1024)}, u32[]{:S(2)}) copy-start(f32[1024]{0:T(1024)} %param.11) | copy-start | bytes 12292
  177.6 71.6 %copy-start.3 = (bf16[16,4,64,128]{3,2,1,0:T(8,128)(2,1)S(1)}, bf16[16,4,64,128]{3,2,1,0:T(8,128)(2,1)}, u32[]{:S(2)}) copy-start(bf16[16,4,64,128]{3,2,1,0:T(8,128)(2,1)} %base_ref.1) | copy-start | bytes 3145732
  177.6 8.6 %collective-permute-start.2 = (f32[32,1024]{1,0:T(8,128)}, f32[32,1024]{1,0:T(8,128)}, u32[]{:S(2)}, u32[]{:S(2)}) collective-permute-start(f32[32,1024]{1,0:T(8,128)} %get-tuple-element.9), channel_id=1, source_target_pairs={{0,1},{1,2},{2,3},{3,4},{4,5},{5,6},{6,7},{7,8},{8,9},{9,10},{10,1... | collective-permute-start | bytes 393224 | tf_op jit(solution)/shard_map/ppermute | solution.py:421
  184.7 3.4 %collective-permute-start.3 = (f32[32,1024]{1,0:T(8,128)S(1)}, f32[32,1024]{1,0:T(8,128)}, u32[]{:S(2)}, u32[]{:S(2)}) collective-permute-start(f32[32,1024]{1,0:T(8,128)S(1)} %get-tuple-element.10), channel_id=1, source_target_pairs={{1,0},{2,1},{3,2},{4,3},{5,4},{6,5},{7,6},{8,7},{9,8},{10,9},{11,1... | collective-permute-start | bytes 393224 | tf_op jit(solution)/shard_map/ppermute | solution.py:421
  189.8 7.8 %all-to-all-start = ((f32[32,2,512]{2,0,1:T(8,128)}), f32[32,2,512]{2,0,1:T(8,128)S(1)}, u32[]{:S(2)}, u32[]{:S(2)}) async-start(f32[32,2,512]{2,0,1:T(8,128)} %bitcast.27), calls=%async_computation | async-start | bytes 262144 | tf_op jit(solution)/shard_map/all_to_all | solution.py:429
  240.2 0.7 copy-start.7
  249.2 2.2 copy-start.2

commit v2 on v1

--- a/solution.py
+++ b/solution.py
@@ -106,7 +106,7 @@
                     )
                 return carry
 
-            lax.fori_loop(0, tiles, body, 0)
+            lax.fori_loop(0, tiles, body, 0, unroll=4)
         for k in range(modes_count):
             r_ref[pl.ds(k * stride + stride - pad, pad), :] = jnp.zeros((pad, lanes), jnp.float32)
 
@@ -120,7 +120,7 @@
                 ].astype(jnp.float32)
             return carry
 
-        lax.fori_loop(0, width // 16, convert, 0)
+        lax.fori_loop(0, width // 16, convert, 0, unroll=4)
 
     def beside(ref, m, at, c, terms):
         total = None
@@ -165,7 +165,7 @@
                 u_ref[m, put, :] = total
             return carry
 
-        lax.fori_loop(0, tiles, second, 0)
+        lax.fori_loop(0, tiles, second, 0, unroll=8)
 
     for z in range(-2, planes + 2):
         if z == -2:
@@ -194,7 +194,7 @@
                 r_ref[pl.ds(put, 8), :] = total
             return carry
 
-        lax.fori_loop(0, tiles, third, 0)
+        lax.fori_loop(0, tiles, third, 0, unroll=8)
 
     @pl.when(step == pl.num_programs(0) - 1)
     def _():
@@ -219,7 +219,7 @@
                     return jnp.where(cols == i, v, acc)
 
                 acc = lax.fori_loop(
-                    0, lanes, one, jnp.zeros((modes_count, lanes), jnp.float32), unroll=8
+                    0, lanes, one, jnp.zeros((modes_count, lanes), jnp.float32), unroll=32
                 )
                 out[:, pl.ds(pl.multiple_of(b * lanes, lanes), lanes)] = acc
                 return carry
@@ -237,7 +237,7 @@
 def stencil(edges, cells, cells_b, cells_a, log_ext, slope, modes):
     modes_count, planes, width, lanes = modes.shape
     count = cells.shape[0]
-    group = 4
+    group = min(8, modes_count)
     n_ext = planes + 2 * REACH + 2
     stride = (planes + 2 * REACH) * width + 8
     smem = pl.BlockSpec(memory_space=pltpu.SMEM)
@@ -268,33 +268,225 @@
     )(edges, cells, cells_b, cells_a, log_ext, slope, modes)
 
 
-def solve_kernel(gram_ref, rhs_ref, out_ref, work):
-    n = gram_ref.shape[0]
-    f = rhs_ref.shape[1]
+def eliminate(matrix, n, block=4):
+    tall = lax.broadcasted_iota(jnp.int32, matrix.shape, 0)
+    for start in range(0, n, block):
+        columns = [
+            jnp.broadcast_to(matrix[:, j : j + 1], matrix.shape)
+            for j in range(start, start + block)
+        ]
+        for i in range(block):
+            j = start + i
+            inverse = 1.0 / columns[i][j : j + 1, :]
+            at = tall == j
+            row = matrix[j : j + 1, :] * inverse
+            matrix = jnp.where(at, row, matrix - columns[i] * row)
+            for k in range(i + 1, block):
+                entry = columns[k][j : j + 1, :] * inverse
+                columns[k] = jnp.where(at, entry, columns[k] - columns[i] * entry)
+    return matrix
+
+
+def stages_of(n_mode, n_slab):
+    stages = []
+    stride = 1
+    while stride < n_slab:
+        radix = next(r for r in (4, 2, 3, n_slab // stride) if (n_slab // stride) % r == 0)
+        stages.append((n_mode if stride == 1 else 1, stride, radix))
+        stride *= radix
+    return stages or [(n_mode, 1, 1)]
+
+
+def reduce_kernel(
+    n_mode, n_slab, stages, own, below, above, var, miss, out,
+    in_b, in_a, picked, whole, sums, work,
+    halo_send, halo_recv, mode_send, mode_recv, sum_send, sum_recv,
+):
+    me = lax.axis_index("mode")
+    slab = lax.axis_index("slab")
+    mine, count = own.shape
+    split = count // n_mode
+    n = mine * n_mode
+    f = miss.shape[1]
+    has_below = slab > 0
+    has_above = slab < n_slab - 1
+    slab_up = jnp.minimum(slab + 1, n_slab - 1)
+    slab_down = jnp.maximum(slab - 1, 0)
+
+    def member(stage, d):
+        modes, stride, radix = stage
+        low = lax.rem(slab // stride, radix)
+        if modes == 1:
+            return me, slab + (lax.rem(low + d, radix) - low) * stride
+        g = lax.rem(me * radix + low + d, modes * radix)
+        return g // radix, slab + (lax.rem(g, radix) - low) * stride
+
+    @pl.when(jnp.logical_not(has_below))
+    def _():
+        in_b[...] = jnp.zeros_like(in_b)
+
+    @pl.when(jnp.logical_not(has_above))
+    def _():
+        in_a[...] = jnp.zeros_like(in_a)
+
+    barrier = pltpu.get_barrier_semaphore()
+
+    def greet(device):
+        pl.semaphore_signal(barrier, inc=1, device_id=device, device_id_type=pl.DeviceIdType.MESH)
+
+    @pl.when(has_above)
+    def _():
+        greet((me, slab_up))
+
+    @pl.when(has_below)
+    def _():
+        greet((me, slab_down))
+
+    greeted = 0
+    for d in range(1, n_mode):
+        greet((lax.rem(me + d, n_mode), slab))
+        greeted += 1
+    for stage in stages:
+        for d in range(1, stage[0] * stage[2]):
+            greet(member(stage, d))
+            greeted += 1
+    ends = jnp.where(has_below, 1, 0) + jnp.where(has_above, 1, 0)
+    pl.semaphore_wait(barrier, greeted + ends)
+
+    def remote(src, dst, send, recv, device):
+        return pltpu.make_async_remote_copy(
+            src_ref=src, dst_ref=dst, send_sem=send, recv_sem=recv,
+            device_id=device, device_id_type=pl.DeviceIdType.MESH,
+        )
+
+    going_up = remote(above, in_b, halo_send.at[0], halo_recv.at[0], (me, slab_up))
+    going_down = remote(below, in_a, halo_send.at[1], halo_recv.at[1], (me, slab_down))
+
+    @pl.when(has_above)
+    def _():
+        going_up.start()
+
+    @pl.when(has_below)
+    def _():
+        going_down.start()
+
+    @pl.when(has_below)
+    def _():
+        going_up.wait_recv()
+
+    @pl.when(has_above)
+    def _():
+        going_down.wait_recv()
+
+    picked[...] = own[...] + in_b[...] + in_a[...]
+
+    copies = []
+    for d in range(1, n_mode):
+        to = lax.rem(me + d, n_mode)
+        piece = pl.ds(pl.multiple_of(to * split, 128), split)
+        copies.append(
+            remote(picked.at[:, piece], whole.at[me], mode_send.at[d], mode_recv.at[d], (to, slab))
+        )
+        copies[-1].start()
+    here = pl.ds(pl.multiple_of(me * split, 128), split)
+    whole[me] = picked[:, here]
+    for copy in copies:
+        copy.wait_recv()
+    every = whole[...].reshape(n, split)
+    scaled = every / var[:, here]
+    gram = lax.dot_general(
+        scaled, every, (((1,), (1,)), ((), ())), precision=lax.Precision.HIGHEST,
+        preferred_element_type=jnp.float32,
+    )
+    rows = pl.ds(pl.multiple_of(me * split, 8), split)
+    rhs = jnp.dot(
+        scaled, miss[rows, :], precision=lax.Precision.HIGHEST, preferred_element_type=jnp.float32
+    )
     work[...] = jnp.zeros_like(work)
-    rows = lax.broadcasted_iota(jnp.int32, (n, n), 0)
-    cols = lax.broadcasted_iota(jnp.int32, (n, n), 1)
-    work[:, :n] = gram_ref[...] + jnp.where(rows == cols, 1.0, 0.0)
-    work[:, n : n + f] = rhs_ref[...]
+    work[:, :n] = gram
+    work[:, n : n + f] = rhs
+
+    base = 0
+    sem = 0
+    for stage in stages:
+        size = stage[0] * stage[2]
+        sums[base] = work[...]
+        moving = []
+        for d in range(1, size):
+            moving.append(
+                remote(sums.at[base], sums.at[base + d], sum_send.at[sem], sum_recv.at[sem],
+                       member(stage, d))
+            )
+            moving[-1].start()
+            sem += 1
+        low = lax.rem(slab // stage[1], stage[2])
+        if stage[0] > 1:
+            low = low + me * stage[2]
+        for copy in moving:
+            copy.wait_recv()
+        total = None
+        for q in range(size):
+            term = sums[base + lax.rem(low - q + size, size)]
+            total = term if total is None else total + term
+        work[...] = total
+        copies += moving
+        base += size
+
     matrix = work[...]
     tall = lax.broadcasted_iota(jnp.int32, matrix.shape, 0)
-    for j in range(n):
-        row = matrix[j : j + 1, :]
-        row = row / row[:, j : j + 1]
-        column = matrix[:, j : j + 1]
-        matrix = jnp.where(tall == j, row, matrix - column * row)
-    work[...] = matrix
-    out_ref[...] = work[:, n : n + f]
-
-
-def solve(gram, rhs):
-    n, f = rhs.shape
+    wide = lax.broadcasted_iota(jnp.int32, matrix.shape, 1)
+    work[...] = eliminate(matrix + jnp.where(tall == wide, 1.0, 0.0), n)
+    for d in range(n_mode):
+        block = lax.rem(me - d + n_mode, n_mode)
+        out[d * mine : (d + 1) * mine, :] = work[
+            pl.ds(pl.multiple_of(block * mine, 8), mine), n : n + f
+        ]
+
+    @pl.when(has_above)
+    def _():
+        going_up.wait_send()
+
+    @pl.when(has_below)
+    def _():
+        going_down.wait_send()
+
+    for copy in copies:
+        copy.wait_send()
+
+
+def reduce_and_solve(own, below, above, obs_var, misfit):
+    n_mode = lax.axis_size("mode")
+    n_slab = lax.axis_size("slab")
+    mine, count = own.shape
+    n = mine * n_mode
+    f = misfit.shape[1]
+    stages = stages_of(n_mode, n_slab)
+    slots = sum(s[0] * s[2] for s in stages)
+    wide = 128 * pl.cdiv(n + f, 128)
+    vmem = pl.BlockSpec(memory_space=pltpu.VMEM)
+    dma = pltpu.SemaphoreType.DMA
     return pl.pallas_call(
-        solve_kernel,
+        functools.partial(reduce_kernel, n_mode, n_slab, stages),
         out_shape=jax.ShapeDtypeStruct((n, f), jnp.float32),
-        scratch_shapes=[pltpu.VMEM((n, 128 * pl.cdiv(n + f, 128)), jnp.float32)],
-        name="solve",
-    )(gram, rhs)
+        in_specs=[vmem] * 5,
+        out_specs=vmem,
+        scratch_shapes=[
+            pltpu.VMEM((mine, count), jnp.float32),
+            pltpu.VMEM((mine, count), jnp.float32),
+            pltpu.VMEM((mine, count), jnp.float32),
+            pltpu.VMEM((n_mode, mine, count // n_mode), jnp.float32),
+            pltpu.VMEM((slots, n, wide), jnp.float32),
+            pltpu.VMEM((n, wide), jnp.float32),
+            dma((2,)), dma((2,)), dma((n_mode,)), dma((n_mode,)), dma((slots,)), dma((slots,)),
+        ],
+        compiler_params=pltpu.CompilerParams(
+            collective_id=0, has_side_effects=True, vmem_limit_bytes=24 * MIB
+        ),
+        cost_estimate=pl.CostEstimate(
+            flops=2 * n * n * count, bytes_accessed=1 << 20, transcendentals=0
+        ),
+        name="reduce_and_solve",
+    )(own, below, above, obs_var.reshape(1, count), misfit)
 
 
 def update_kernel(place_ref, coef_ref, own_ref, others_ref, base_ref, out_ref, big):
@@ -418,33 +610,8 @@
     cells_a = from_above[halo * width :].reshape(-1).astype(jnp.int32)
     edges = jnp.stack([level == 0, level == n_slab - 1]).astype(jnp.int32)
     own, below, above = stencil(edges, obs_cells, cells_b, cells_a, log_ext, head_slope, modes)
-    picked = own + lax.ppermute(above, "slab", up) + lax.ppermute(below, "slab", down)
-    return picked, others, me
-
-
-def finish(own, others, me, modes, obs_var, misfit, base_fields):
-    n_mode = lax.axis_size("mode")
-    mine = modes.shape[0]
-    split = own.shape[1] // n_mode
-    whole = lax.all_to_all(own, "mode", split_axis=1, concat_axis=0, tiled=True)
-    var = lax.dynamic_slice_in_dim(obs_var, me * split, split, axis=0)
-    miss = lax.dynamic_slice_in_dim(misfit, me * split, split, axis=0)
-    scaled = whole / var[None, :]
-    right = jnp.concatenate([whole.T, miss], axis=1)
-    both = jnp.dot(scaled, right, precision=lax.Precision.HIGHEST)
-    both = lax.psum(both, ("mode", "slab"))
-    total = mine * n_mode
-    coef = solve(both[:, :total], both[:, total:])
-    order = (me - jnp.arange(n_mode)) % n_mode
-    coef = coef.reshape(n_mode, mine, -1)[order].reshape(total, -1)
+    coef = reduce_and_solve(own, below, above, obs_var, misfit)
     return update(me.astype(jnp.int32).reshape(1), coef, modes, others, base_fields)
-
-
-def both_phases(log_cond, head_slope, modes, obs_cells, obs_var, misfit, base_fields):
-    picked, others, me = on_device(
-        log_cond, head_slope, modes, obs_cells, obs_var, misfit, base_fields
-    )
-    return finish(picked, others, me, modes, obs_var, misfit, base_fields)
 
 
 def solution(mesh):
@@ -458,7 +625,7 @@
         P(None, "slab", "mode", None),
     )
     return jax.shard_map(
-        both_phases,
+        on_device,
         mesh=mesh,
         in_specs=placed,
         out_specs=P(None, "slab", "mode", None),

time: 258 us -> 93.5 us (0.36)
  Pallas kernels: 176 us -> 77.3 us
  blocking collectives: 42.2 us -> 0 us
  starting transfers between devices: 17.5 us -> 5.69 us
  waiting for transfers between devices: 9.92 us -> 2.68 us
  local copies, waits for them, and re-layouts: 10.4 us -> 6.54 us
    pallas_call x1, Pallas kernels: 163 us -> 44.7 us  [stencil(): pl.pallas_call(functools.partial(stencil_kernel, planes, width, modes_cou...]
    psum x1 -> x0, blocking collectives: 42.2 us -> none  [finish(): both = lax.psum(both, ('mode', 'slab'))]
    pallas_call x1, Pallas kernels: 6.95 us -> 26.4 us  [reduce_and_solve(): pl.pallas_call(functools.partial(reduce_kernel, n_mode, n_slab, stages),...]
    ppermute x2 -> x0, starting transfers between devices: 8.45 us -> none  [the longest x1 7.17 us: on_device(): lax.ppermute(above, 'slab', up)]
    all_to_all x1 -> x0, waiting for transfers between devices: 4.44 us -> none  [finish(): whole = lax.all_to_all(own, 'mode', split_axis=1, concat_axis=0, tiled=True)]
    all_to_all x1 -> x0, starting transfers between devices: 3.38 us -> none  [finish(): whole = lax.all_to_all(own, 'mode', split_axis=1, concat_axis=0, tiled=True)]
  transfers between devices with their start and end apart: 6 -> 3, of which waited for: 3 -> 1; matrix products, arithmetic and copies ran while one was open for 2% -> 2% of each run, Pallas kernels for 66% -> 76%
where the time goes in v2:
time: 93.5 us; the launch traced here: 93.3 us
  Pallas kernels  77.3 us (83%)
  local copies, waits for them, and re-layouts  6.54 us (7%)
  starting transfers between devices  5.69 us (6%)
  waiting for transfers between devices  2.68 us (3%)
    pallas_call x1, Pallas kernels, stencil(): pl.pallas_call(functools.partial(stencil_kernel, planes, width, modes_cou...  44.7 us
    pallas_call x1, Pallas kernels, reduce_and_solve(): pl.pallas_call(functools.partial(reduce_kernel, n_mode, n_slab, stages),...  26.4 us
    pallas_call x1, Pallas kernels, update(): pl.pallas_call(update_kernel, grid_spec=pltpu.PrefetchScalarGridSpec(num_...  6.28 us
    dynamic_slice x1, local copies, waits for them, and re-layouts, on_device(): piece = lax.dynamic_slice_in_dim(modes, to * part, part, axis=2)  3.24 us
    unnamed x13, local copies, waits for them, and re-layouts  3.24 us
    ppermute x1, starting transfers between devices, on_device(): lax.ppermute(piece, 'mode', [(i, (i + d) % n_mode) for i in range(n_mode)])  2.94 us
    ppermute x1, waiting for transfers between devices, on_device(): from_above = lax.ppermute(message(log_cond[:halo]), 'slab', down)  2.67 us
  transfers between devices with their start and end apart: 3, of which 1 were waited for; matrix products, arithmetic and copies ran while one was open for 2% of the time, Pallas kernels for 76%

profile of v2, /device:TPU:0, one launch (start us, length us, event | category | flops | bytes accessed | tf_op | source)
XLA Modules:
  0.0 93.3 jit_solution(16208950839522191600)
XLA Ops:
  0.0 0.0 copy-start.3
  0.0 0.0 copy-start.5
  0.0 3.2 %constant_dynamic-slice_fusion = bf16[32,4,64,128]{3,2,1,0:T(8,128)(2,1)} fusion(bf16[32,4,128,128]{3,2,1,0:T(8,128)(2,1)} %own_ref.1, s32[]{:T(128)S(6)} %select_n.11), kind=kLoop, calls=%fused_computation.9 | loop fusion | bytes 4194308 | tf_op jit(solution)/shard_map/dynamic_slice | solution.py:585
  3.2 2.9 %collective-permute-start.2 = (bf16[32,4,64,128]{3,2,1,0:T(8,128)(2,1)}, bf16[32,4,64,128]{3,2,1,0:T(8,128)(2,1)S(1)}, u32[]{:S(2)}, u32[]{:S(2)}) collective-permute-start(bf16[32,4,64,128]{3,2,1,0:T(8,128)(2,1)} %constant_dynamic-slice_fusion), channel_id=1, source_target_pairs={{0,16},{16,0},{1,17},{17,1},{2,18},{18,2},{3,19},{19,3},{4,20},{20... | collective-permute-start | bytes 6291464 | tf_op jit(solution)/shard_map/ppermute | solution.py:587
  6.2 0.0 copy-done.3
  6.2 0.0 copy-done.5
  6.2 0.0 copy-start.2
  6.2 0.8 pad_maximum_fusion.1
  7.0 1.5 %collective-permute-start = (f32[392,128]{1,0:T(8,128)}, f32[392,128]{1,0:T(8,128)S(1)}, u32[]{:S(2)}, u32[]{:S(2)}) collective-permute-start(f32[392,128]{1,0:T(8,128)} %get-tuple-element.14), channel_id=1, source_target_pairs={{0,1},{1,2},{2,3},{3,4},{4,5},{5,6},{6,7},{7,8},{8,9},{9,10},{10,1... | collective-permute-start | bytes 602120 | tf_op jit(solution)/shard_map/ppermute | solution.py:599
  8.5 1.3 %collective-permute-start.1 = (f32[392,128]{1,0:T(8,128)}, f32[392,128]{1,0:T(8,128)S(1)}, u32[]{:S(2)}, u32[]{:S(2)}) collective-permute-start(f32[392,128]{1,0:T(8,128)} %get-tuple-element.13), channel_id=1, source_target_pairs={{1,0},{2,1},{3,2},{4,3},{5,4},{6,5},{7,6},{8,7},{9,8},{10,9},{11,1... | collective-permute-start | bytes 602120 | tf_op jit(solution)/shard_map/ppermute | solution.py:600
  9.8 1.0 %copy.8.miss = f32[1024,16]{1,0:T(8,128)S(1)} copy(f32[1024,16]{0,1:T(8,128)} %param.12) | data formatting | bytes 131072 | tf_op args[5]
  10.8 0.1 add_convert_fusion.edge_ref
  10.9 0.0 collective-permute-done
  10.9 2.7 %collective-permute-done.1 = f32[392,128]{1,0:T(8,128)S(1)} collective-permute-done((f32[392,128]{1,0:T(8,128)}, f32[392,128]{1,0:T(8,128)S(1)}, u32[]{:S(2)}, u32[]{:S(2)}) %collective-permute-start.1) | collective-permute-done | bytes 200736 | tf_op jit(solution)/shard_map/ppermute | solution.py:600
  13.7 0.0 copy-done.2
  13.7 0.0 copy-start
  13.7 2.2 %copy-done = bf16[32,4,128,128]{3,2,1,0:T(8,128)(2,1)S(1)} copy-done((bf16[32,4,128,128]{3,2,1,0:T(8,128)(2,1)S(1)}, bf16[32,4,128,128]{3,2,1,0:T(8,128)(2,1)}, u32[]{:S(2)}) %copy-start) | copy-done | bytes 4194328
  15.9 0.0 copy-start.4
  15.9 0.0 copy-start.1
  15.9 44.7 %stencil.1 = (f32[32,1024]{1,0:T(8,128)S(1)}, f32[32,1024]{1,0:T(8,128)S(1)}, f32[32,1024]{1,0:T(8,128)S(1)}) custom-call(s32[2]{0:T(128)S(1)} %add_convert_fusion.edge_ref, s32[1024]{0:T(1024)S(1)} %copy-done.3, s32[1024]{0:T(1024)S(1)} %fusion.1.cells_b_ref, s32[1024]{0:T(1024)S(1)} %fusion.cells_a_ref, f32[10,128,128]{2,1,0:T(8,128)S(1)} %pad_maximum_fusion.log_ref, ...), custom_call_target="tpu_custom_call" | custom-call | flops 83886080 | bytes 8388608 | tf_op jit(solution)/shard_map/stencil/pallas_call | solution.py:246
  60.6 0.0 copy-done.4
  60.6 26.4 %reduce_and_solve.1.coef_ref = f32[64,16]{1,0:T(8,128)S(1)} custom-call(f32[32,1024]{1,0:T(8,128)S(1)} %get-tuple-element.8.own, f32[32,1024]{1,0:T(8,128)S(1)} %get-tuple-element.9.below, f32[32,1024]{1,0:T(8,128)S(1)} %get-tuple-element.10.above, f32[1,1024]{1,0:T(1,128)S(1)} %bitcast.14, f32[1024,16]{1,0:T(8,128)S(1)} %copy.8.miss), custom_call_target="tpu_custom_call" | custom-call | flops 8388608 | bytes 1048576 | tf_op jit(solution)/shard_map/reduce_and_solve/pallas_call | solution.py:468
  87.0 0.0 collective-permute-done.2.others_ref
  87.0 0.0 copy-done.1
  87.0 6.3 %update.1 = f32[16,4,64,128]{3,2,1,0:T(8,128)} custom-call(s32[1]{0:T(128)} %bitcast.place_ref, f32[64,16]{1,0:T(8,128)S(1)} %reduce_and_solve.1.coef_ref, bf16[32,4,128,128]{3,2,1,0:T(8,128)(2,1)S(1)} %copy-done, bf16[32,4,64,128]{3,2,1,0:T(8,128)(2,1)S(1)} %collective-permute-done.2.others_ref, bf16[16,4,64,128]{3,2,1,0:T(8,128)(2,1)S(1)} %copy-done.1), custom_call_target="tpu_custom_call" | custom-call | tf_op jit(solution)/shard_map/update/pallas_call | solution.py:547
  (7 shorter events, 0.1 us)
Async XLA Ops:
  0.0 6.2 %copy-start.3 = (s32[1024]{0:T(1024)S(1)}, s32[1024]{0:T(1024)}, u32[]{:S(2)}) copy-start(s32[1024]{0:T(1024)} %cells_ref.1) | copy-start | bytes 12292
  0.0 6.2 %copy-start.5 = (f32[4,128,128]{2,1,0:T(8,128)S(1)}, f32[4,128,128]{2,1,0:T(8,128)}, u32[]{:S(2)}) copy-start(f32[4,128,128]{2,1,0:T(8,128)} %param.7) | copy-start | bytes 786436
  3.2 83.7 %collective-permute-start.2 = (bf16[32,4,64,128]{3,2,1,0:T(8,128)(2,1)}, bf16[32,4,64,128]{3,2,1,0:T(8,128)(2,1)S(1)}, u32[]{:S(2)}, u32[]{:S(2)}) collective-permute-start(bf16[32,4,64,128]{3,2,1,0:T(8,128)(2,1)} %constant_dynamic-slice_fusion), channel_id=1, source_target_pairs={{0,16},{16,0},{1,17},{17,1},{2,18},{18,2},{3,19},{19,3},{4,20},{20... | collective-permute-start | bytes 6291464 | tf_op jit(solution)/shard_map/ppermute | solution.py:587
  6.2 7.5 %copy-start.2 = (f32[4,128,128]{2,1,0:T(8,128)S(1)}, f32[4,128,128]{2,1,0:T(8,128)}, u32[]{:S(2)}) copy-start(f32[4,128,128]{2,1,0:T(8,128)} %slope_ref.1) | copy-start | bytes 786436
  7.0 3.9 %collective-permute-start = (f32[392,128]{1,0:T(8,128)}, f32[392,128]{1,0:T(8,128)S(1)}, u32[]{:S(2)}, u32[]{:S(2)}) collective-permute-start(f32[392,128]{1,0:T(8,128)} %get-tuple-element.14), channel_id=1, source_target_pairs={{0,1},{1,2},{2,3},{3,4},{4,5},{5,6},{6,7},{7,8},{8,9},{9,10},{10,1... | collective-permute-start | bytes 602120 | tf_op jit(solution)/shard_map/ppermute | solution.py:599
  8.5 5.1 %collective-permute-start.1 = (f32[392,128]{1,0:T(8,128)}, f32[392,128]{1,0:T(8,128)S(1)}, u32[]{:S(2)}, u32[]{:S(2)}) collective-permute-start(f32[392,128]{1,0:T(8,128)} %get-tuple-element.13), channel_id=1, source_target_pairs={{1,0},{2,1},{3,2},{4,3},{5,4},{6,5},{7,6},{8,7},{9,8},{10,9},{11,1... | collective-permute-start | bytes 602120 | tf_op jit(solution)/shard_map/ppermute | solution.py:600
  13.7 2.2 %copy-start = (bf16[32,4,128,128]{3,2,1,0:T(8,128)(2,1)S(1)}, bf16[32,4,128,128]{3,2,1,0:T(8,128)(2,1)}, u32[]{:S(2)}) copy-start(bf16[32,4,128,128]{3,2,1,0:T(8,128)(2,1)} %own_ref.1) | copy-start | bytes 12582916
  15.9 44.7 %copy-start.4 = (f32[1024]{0:T(1024)S(1)}, f32[1024]{0:T(1024)}, u32[]{:S(2)}) copy-start(f32[1024]{0:T(1024)} %param.11) | copy-start | bytes 12292
  15.9 71.1 %copy-start.1 = (bf16[16,4,64,128]{3,2,1,0:T(8,128)(2,1)S(1)}, bf16[16,4,64,128]{3,2,1,0:T(8,128)(2,1)}, u32[]{:S(2)}) copy-start(bf16[16,4,64,128]{3,2,1,0:T(8,128)(2,1)} %base_ref.1) | copy-start | bytes 3145732

commit v3 on v2

--- a/solution.py
+++ b/solution.py
@@ -12,6 +12,7 @@
 STORAGE = 0.05
 REACH = ITERS - 1
 MIB = 1 << 20
+ROWS = 8
 
 
 def sweep_weights(count):
@@ -106,7 +107,7 @@
                     )
                 return carry
 
-            lax.fori_loop(0, tiles, body, 0, unroll=4)
+            lax.fori_loop(0, tiles, body, 0, unroll=8)
         for k in range(modes_count):
             r_ref[pl.ds(k * stride + stride - pad, pad), :] = jnp.zeros((pad, lanes), jnp.float32)
 
@@ -120,7 +121,7 @@
                 ].astype(jnp.float32)
             return carry
 
-        lax.fori_loop(0, width // 16, convert, 0, unroll=4)
+        lax.fori_loop(0, width // 16, convert, 0, unroll=8)
 
     def beside(ref, m, at, c, terms):
         total = None
@@ -165,7 +166,7 @@
                 u_ref[m, put, :] = total
             return carry
 
-        lax.fori_loop(0, tiles, second, 0, unroll=8)
+        lax.fori_loop(0, tiles, second, 0, unroll=tiles)
 
     for z in range(-2, planes + 2):
         if z == -2:
@@ -194,7 +195,7 @@
                 r_ref[pl.ds(put, 8), :] = total
             return carry
 
-        lax.fori_loop(0, tiles, third, 0, unroll=8)
+        lax.fori_loop(0, tiles, third, 0, unroll=tiles)
 
     @pl.when(step == pl.num_programs(0) - 1)
     def _():
@@ -219,7 +220,7 @@
                     return jnp.where(cols == i, v, acc)
 
                 acc = lax.fori_loop(
-                    0, lanes, one, jnp.zeros((modes_count, lanes), jnp.float32), unroll=32
+                    0, lanes, one, jnp.zeros((modes_count, lanes), jnp.float32), unroll=lanes
                 )
                 out[:, pl.ds(pl.multiple_of(b * lanes, lanes), lanes)] = acc
                 return carry
@@ -259,7 +260,7 @@
             pltpu.VMEM((modes_count * stride, lanes), jnp.float32),
         ],
         compiler_params=pltpu.CompilerParams(
-            dimension_semantics=("arbitrary",), vmem_limit_bytes=40 * MIB
+            dimension_semantics=("arbitrary",), vmem_limit_bytes=46 * MIB
         ),
         cost_estimate=pl.CostEstimate(
             flops=40 * modes.size, bytes_accessed=4 * modes.size, transcendentals=0
@@ -307,7 +308,7 @@
     mine, count = own.shape
     split = count // n_mode
     n = mine * n_mode
-    f = miss.shape[1]
+    f = miss.shape[0]
     has_below = slab > 0
     has_above = slab < n_slab - 1
     slab_up = jnp.minimum(slab + 1, n_slab - 1)
@@ -398,9 +399,9 @@
         scaled, every, (((1,), (1,)), ((), ())), precision=lax.Precision.HIGHEST,
         preferred_element_type=jnp.float32,
     )
-    rows = pl.ds(pl.multiple_of(me * split, 8), split)
-    rhs = jnp.dot(
-        scaled, miss[rows, :], precision=lax.Precision.HIGHEST, preferred_element_type=jnp.float32
+    rhs = lax.dot_general(
+        scaled, miss[:, here], (((1,), (1,)), ((), ())), precision=lax.Precision.HIGHEST,
+        preferred_element_type=jnp.float32,
     )
     work[...] = jnp.zeros_like(work)
     work[:, :n] = gram
@@ -486,7 +487,7 @@
             flops=2 * n * n * count, bytes_accessed=1 << 20, transcendentals=0
         ),
         name="reduce_and_solve",
-    )(own, below, above, obs_var.reshape(1, count), misfit)
+    )(own, below, above, obs_var.reshape(1, count), misfit.T)
 
 
 def update_kernel(place_ref, coef_ref, own_ref, others_ref, base_ref, out_ref, big):
@@ -499,16 +500,16 @@
         coef = coef_ref[...]
         high = coef.astype(jnp.bfloat16)
         low = (coef - high.astype(jnp.float32)).astype(jnp.bfloat16)
-        tall, wide = fields * rows, total * rows
+        tall, wide = fields * ROWS, total * ROWS
         r0 = lax.broadcasted_iota(jnp.int32, (tall, fields), 0)
         f0 = lax.broadcasted_iota(jnp.int32, (tall, fields), 1)
-        spread_f = jnp.where(r0 // rows == f0, 1.0, 0.0).astype(jnp.bfloat16)
+        spread_f = jnp.where(r0 // ROWS == f0, 1.0, 0.0).astype(jnp.bfloat16)
         k0 = lax.broadcasted_iota(jnp.int32, (total, wide), 0)
         c0 = lax.broadcasted_iota(jnp.int32, (total, wide), 1)
-        spread_k = jnp.where(c0 // rows == k0, 1.0, 0.0).astype(jnp.bfloat16)
+        spread_k = jnp.where(c0 // ROWS == k0, 1.0, 0.0).astype(jnp.bfloat16)
         r1 = lax.broadcasted_iota(jnp.int32, (tall, wide), 0)
         c1 = lax.broadcasted_iota(jnp.int32, (tall, wide), 1)
-        same = r1 % rows == c1 % rows
+        same = r1 % ROWS == c1 % ROWS
         for p, part in enumerate((high, low)):
             a = lax.dot_general(
                 spread_f, part, (((1,), (1,)), ((), ())), preferred_element_type=jnp.float32
@@ -516,21 +517,30 @@
             b = jnp.dot(a, spread_k, preferred_element_type=jnp.float32)
             big[p * tall : (p + 1) * tall, :] = jnp.where(same, b, 0.0).astype(jnp.bfloat16)
 
-    tall = fields * rows
-    left = mine * rows
+    tall = fields * ROWS
+    left = mine * ROWS
 
     def side(ref):
         count = ref.shape[0]
-        return jnp.concatenate(
-            [ref[:, d].reshape(count * rows, lanes) for d in range(deep)], axis=1
-        )
+        tiles = []
+        for d in range(deep):
+            whole = ref[:, d].astype(jnp.float32)
+            for h in range(rows // ROWS):
+                tile = whole[:, h * ROWS : (h + 1) * ROWS, :]
+                tiles.append(tile.reshape(count * ROWS, lanes).astype(jnp.bfloat16))
+        return jnp.concatenate(tiles, axis=1)
 
     both = jnp.dot(big[:, :left], side(own_ref), preferred_element_type=jnp.float32)
     both = both + jnp.dot(big[:, left:], side(others_ref), preferred_element_type=jnp.float32)
     both = both[:tall] + both[tall:]
     for d in range(deep):
-        part = both[:, d * lanes : (d + 1) * lanes].reshape(fields, rows, lanes)
-        out_ref[:, d] = base_ref[:, d].astype(jnp.float32) + part
+        base = base_ref[:, d].astype(jnp.float32)
+        for h in range(rows // ROWS):
+            at = (d * (rows // ROWS) + h) * lanes
+            part = both[:, at : at + lanes].reshape(fields, ROWS, lanes)
+            out_ref[:, d, h * ROWS : (h + 1) * ROWS, :] = (
+                base[:, h * ROWS : (h + 1) * ROWS, :] + part
+            )
 
 
 def update(place, coef, modes, others, base):
@@ -560,7 +570,7 @@
             ],
             out_specs=fixed(fields),
             scratch_shapes=[
-                pltpu.VMEM((2 * fields * rows, (mine + rest) * rows), jnp.bfloat16)
+                pltpu.VMEM((2 * fields * ROWS, (mine + rest) * ROWS), jnp.bfloat16)
             ],
         ),
         out_shape=jax.ShapeDtypeStruct(base.shape, jnp.float32),
@@ -579,6 +589,19 @@
     level = lax.axis_index("slab")
     part = width // n_mode
 
+    up = [(i, i + 1) for i in range(n_slab - 1)]
+    down = [(i + 1, i) for i in range(n_slab - 1)]
+    halo = REACH + 1
+    cells_f = obs_cells.astype(jnp.float32).reshape(-1, lanes)
+
+    def message(planes_out):
+        return jnp.concatenate([planes_out.reshape(-1, lanes), cells_f], axis=0)
+
+    to_above, to_below, modes = lax.optimization_barrier(
+        (message(log_cond[-halo:]), message(log_cond[:halo]), modes)
+    )
+    from_below = lax.ppermute(to_above, "slab", up)
+    from_above = lax.ppermute(to_below, "slab", down)
     received = []
     for d in range(1, n_mode):
         to = (me + d) % n_mode
@@ -588,16 +611,6 @@
         )
     others = received[0] if n_mode == 2 else jnp.concatenate(received, axis=0)
 
-    up = [(i, i + 1) for i in range(n_slab - 1)]
-    down = [(i + 1, i) for i in range(n_slab - 1)]
-    halo = REACH + 1
-    cells_f = obs_cells.astype(jnp.float32).reshape(-1, lanes)
-
-    def message(planes_out):
-        return jnp.concatenate([planes_out.reshape(-1, lanes), cells_f], axis=0)
-
-    from_below = lax.ppermute(message(log_cond[-halo:]), "slab", up)
-    from_above = lax.ppermute(message(log_cond[:halo]), "slab", down)
     log_ext = jnp.concatenate(
         [
             from_below[: halo * width].reshape(halo, width, lanes),

time: 93.5 us -> 81.2 us (0.87)
  Pallas kernels: 77.3 us -> 64.2 us
    pallas_call x1, Pallas kernels: 44.7 us -> 32.5 us  [stencil(): pl.pallas_call(functools.partial(stencil_kernel, planes, width, modes_cou...]
    unnamed x13 -> x14, local copies, waits for them, and re-layouts: 3.24 us -> 2.21 us
    slice x1, local copies, waits for them, and re-layouts: 0.03 us -> 1.05 us  [on_device(): log_cond[:halo]]
  transfers between devices with their start and end apart: 3 -> 3, of which waited for: 1 -> 1; matrix products, arithmetic and copies ran while one was open for 2% -> 0% of each run, Pallas kernels for 76% -> 73%
where the time goes in v3:
time: 81.2 us; the launch traced here: 80.9 us
  Pallas kernels  64.2 us (79%)
  local copies, waits for them, and re-layouts  6.53 us (8%)
  starting transfers between devices  5.69 us (7%)
  waiting for transfers between devices  3.52 us (4%)
  other arithmetic  0.85 us (1%)
    pallas_call x1, Pallas kernels, stencil(): pl.pallas_call(functools.partial(stencil_kernel, planes, width, modes_cou...  32.5 us
    pallas_call x1, Pallas kernels, reduce_and_solve(): pl.pallas_call(functools.partial(reduce_kernel, n_mode, n_slab, stages),...  26.3 us
    pallas_call x1, Pallas kernels, update(): pl.pallas_call(update_kernel, grid_spec=pltpu.PrefetchScalarGridSpec(num_...  5.37 us
    ppermute x1, waiting for transfers between devices, on_device(): from_above = lax.ppermute(to_below, 'slab', down)  3.51 us
    dynamic_slice x1, local copies, waits for them, and re-layouts, on_device(): piece = lax.dynamic_slice_in_dim(modes, to * part, part, axis=2)  3.25 us
    ppermute x1, starting transfers between devices, on_device(): lax.ppermute(piece, 'mode', [(i, (i + d) % n_mode) for i in range(n_mode)])  2.94 us
    unnamed x14, local copies, waits for them, and re-layouts  2.21 us
  transfers between devices with their start and end apart: 3, of which 1 were waited for; matrix products, arithmetic and copies ran while one was open for 0% of the time, Pallas kernels for 73%

profile of v3, /device:TPU:0, one launch (start us, length us, event | category | flops | bytes accessed | tf_op | source)
XLA Modules:
  0.0 80.9 jit_solution(1426103832907792880)
XLA Ops:
  0.0 0.7 convert_bitcast_fusion
  0.7 1.0 %fusion.2 = (f32[3,128,128]{2,1,0:T(8,128)S(1)}, f32[3,128,128]{2,1,0:T(8,128)S(1)}) fusion(f32[4,128,128]{2,1,0:T(8,128)} %param.7), kind=kLoop, calls=%fused_computation.10 | loop fusion | bytes 786432 | tf_op jit(solution)/shard_map/slice | solution.py:601
  1.8 0.0 copy-start.6
  1.8 3.3 %constant_dynamic-slice_fusion = bf16[32,4,64,128]{3,2,1,0:T(8,128)(2,1)} fusion(bf16[32,4,128,128]{3,2,1,0:T(8,128)(2,1)} %own_ref, s32[]{:T(128)S(6)} %select_n.11), kind=kLoop, calls=%fused_computation.9 | loop fusion | bytes 4194308 | tf_op jit(solution)/shard_map/dynamic_slice | solution.py:608
  5.0 0.0 copy-start.2
  5.0 0.0 copy-start.4
  5.0 2.9 %collective-permute-start.2 = (bf16[32,4,64,128]{3,2,1,0:T(8,128)(2,1)}, bf16[32,4,64,128]{3,2,1,0:T(8,128)(2,1)S(1)}, u32[]{:S(2)}, u32[]{:S(2)}) collective-permute-start(bf16[32,4,64,128]{3,2,1,0:T(8,128)(2,1)} %constant_dynamic-slice_fusion), channel_id=1, source_target_pairs={{0,16},{16,0},{1,17},{17,1},{2,18},{18,2},{3,19},{19,3},{4,20},{20... | collective-permute-start | bytes 6291464 | tf_op jit(solution)/shard_map/ppermute | solution.py:610
  8.0 1.5 %collective-permute-start = (f32[392,128]{1,0:T(8,128)S(1)}, f32[392,128]{1,0:T(8,128)S(1)}, u32[]{:S(2)}, u32[]{:S(2)}) collective-permute-start(f32[392,128]{1,0:T(8,128)S(1)} %get-tuple-element.11), channel_id=1, source_target_pairs={{0,1},{1,2},{2,3},{3,4},{4,5},{5,6},{6,7},{7,8},{8,9},{9,10},{10,1... | collective-permute-start | bytes 602120 | tf_op jit(solution)/shard_map/ppermute | solution.py:603
  9.5 1.3 %collective-permute-start.1 = (f32[392,128]{1,0:T(8,128)S(1)}, f32[392,128]{1,0:T(8,128)S(1)}, u32[]{:S(2)}, u32[]{:S(2)}) collective-permute-start(f32[392,128]{1,0:T(8,128)S(1)} %get-tuple-element.12), channel_id=1, source_target_pairs={{1,0},{2,1},{3,2},{4,3},{5,4},{6,5},{7,6},{8,7},{9,8},{10,9},{11,1... | collective-permute-start | bytes 602120 | tf_op jit(solution)/shard_map/ppermute | solution.py:604
  10.8 0.1 add_convert_fusion.edge_ref
  10.8 0.0 collective-permute-done
  10.9 3.5 %collective-permute-done.1 = f32[392,128]{1,0:T(8,128)S(1)} collective-permute-done((f32[392,128]{1,0:T(8,128)S(1)}, f32[392,128]{1,0:T(8,128)S(1)}, u32[]{:S(2)}, u32[]{:S(2)}) %collective-permute-start.1) | collective-permute-done | bytes 200736 | tf_op jit(solution)/shard_map/ppermute | solution.py:604
  14.4 0.0 copy-done.6
  14.5 0.0 copy-done.2
  14.5 0.0 copy-done.4
  14.5 0.0 copy-start
  14.5 2.2 %copy-done = bf16[32,4,128,128]{3,2,1,0:T(8,128)(2,1)S(1)} copy-done((bf16[32,4,128,128]{3,2,1,0:T(8,128)(2,1)S(1)}, bf16[32,4,128,128]{3,2,1,0:T(8,128)(2,1)}, u32[]{:S(2)}) %copy-start) | copy-done | bytes 4194328
  16.7 0.0 copy-start.3
  16.7 0.0 copy-start.5
  16.7 0.0 copy-start.1
  16.7 32.5 %stencil.1 = (f32[32,1024]{1,0:T(8,128)S(1)}, f32[32,1024]{1,0:T(8,128)S(1)}, f32[32,1024]{1,0:T(8,128)S(1)}) custom-call(s32[2]{0:T(128)S(1)} %add_convert_fusion.edge_ref, s32[1024]{0:T(1024)S(1)} %copy-done.4, s32[1024]{0:T(1024)S(1)} %fusion.1.cells_b_ref, s32[1024]{0:T(1024)S(1)} %fusion.cells_a_ref, f32[10,128,128]{2,1,0:T(8,128)S(1)} %pad_maximum_fusion.log_ref, ...), custom_call_target="tpu_custom_call" | custom-call | flops 83886080 | bytes 8388608 | tf_op jit(solution)/shard_map/stencil/pallas_call | solution.py:247
  49.2 0.0 copy-done.3
  49.2 0.0 copy-done.5
  49.2 26.3 %reduce_and_solve.1.coef_ref = f32[64,16]{1,0:T(8,128)S(1)} custom-call(f32[32,1024]{1,0:T(8,128)S(1)} %get-tuple-element.14.own, f32[32,1024]{1,0:T(8,128)S(1)} %get-tuple-element.15.below, f32[32,1024]{1,0:T(8,128)S(1)} %get-tuple-element.16.above, f32[1,1024]{1,0:T(1,128)S(1)} %bitcast.16, f32[16,1024]{1,0:T(8,128)S(1)} %bitcast.15), custom_call_target="tpu_custom_call" | custom-call | flops 8388608 | bytes 1048576 | tf_op jit(solution)/shard_map/reduce_and_solve/pallas_call | solution.py:469
  75.6 0.0 collective-permute-done.2.others_ref
  75.6 0.0 copy-done.1
  75.6 5.4 %update.1 = f32[16,4,64,128]{3,2,1,0:T(8,128)} custom-call(s32[1]{0:T(128)} %bitcast.place_ref, f32[64,16]{1,0:T(8,128)S(1)} %reduce_and_solve.1.coef_ref, bf16[32,4,128,128]{3,2,1,0:T(8,128)(2,1)S(1)} %copy-done, bf16[32,4,64,128]{3,2,1,0:T(8,128)(2,1)S(1)} %collective-permute-done.2.others_ref, bf16[16,4,64,128]{3,2,1,0:T(8,128)(2,1)S(1)} %copy-done.1), custom_call_target="tpu_custom_call" | custom-call | tf_op jit(solution)/shard_map/update/pallas_call | solution.py:557
  (6 shorter events, 0.1 us)
Async XLA Ops:
  1.8 12.6 %copy-start.6 = (f32[4,128,128]{2,1,0:T(8,128)S(1)}, f32[4,128,128]{2,1,0:T(8,128)}, u32[]{:S(2)}) copy-start(f32[4,128,128]{2,1,0:T(8,128)} %param.7) | copy-start | bytes 786436
  5.0 9.4 %copy-start.2 = (f32[4,128,128]{2,1,0:T(8,128)S(1)}, f32[4,128,128]{2,1,0:T(8,128)}, u32[]{:S(2)}) copy-start(f32[4,128,128]{2,1,0:T(8,128)} %slope_ref.1) | copy-start | bytes 786436
  5.0 9.4 %copy-start.4 = (s32[1024]{0:T(1024)S(1)}, s32[1024]{0:T(1024)}, u32[]{:S(2)}) copy-start(s32[1024]{0:T(1024)} %cells_ref.1) | copy-start | bytes 12292
  5.0 70.5 %collective-permute-start.2 = (bf16[32,4,64,128]{3,2,1,0:T(8,128)(2,1)}, bf16[32,4,64,128]{3,2,1,0:T(8,128)(2,1)S(1)}, u32[]{:S(2)}, u32[]{:S(2)}) collective-permute-start(bf16[32,4,64,128]{3,2,1,0:T(8,128)(2,1)} %constant_dynamic-slice_fusion), channel_id=1, source_target_pairs={{0,16},{16,0},{1,17},{17,1},{2,18},{18,2},{3,19},{19,3},{4,20},{20... | collective-permute-start | bytes 6291464 | tf_op jit(solution)/shard_map/ppermute | solution.py:610
  8.0 2.9 %collective-permute-start = (f32[392,128]{1,0:T(8,128)S(1)}, f32[392,128]{1,0:T(8,128)S(1)}, u32[]{:S(2)}, u32[]{:S(2)}) collective-permute-start(f32[392,128]{1,0:T(8,128)S(1)} %get-tuple-element.11), channel_id=1, source_target_pairs={{0,1},{1,2},{2,3},{3,4},{4,5},{5,6},{6,7},{7,8},{8,9},{9,10},{10,1... | collective-permute-start | bytes 602120 | tf_op jit(solution)/shard_map/ppermute | solution.py:603
  9.5 4.9 %collective-permute-start.1 = (f32[392,128]{1,0:T(8,128)S(1)}, f32[392,128]{1,0:T(8,128)S(1)}, u32[]{:S(2)}, u32[]{:S(2)}) collective-permute-start(f32[392,128]{1,0:T(8,128)S(1)} %get-tuple-element.12), channel_id=1, source_target_pairs={{1,0},{2,1},{3,2},{4,3},{5,4},{6,5},{7,6},{8,7},{9,8},{10,9},{11,1... | collective-permute-start | bytes 602120 | tf_op jit(solution)/shard_map/ppermute | solution.py:604
  14.5 2.2 %copy-start = (bf16[32,4,128,128]{3,2,1,0:T(8,128)(2,1)S(1)}, bf16[32,4,128,128]{3,2,1,0:T(8,128)(2,1)}, u32[]{:S(2)}) copy-start(bf16[32,4,128,128]{3,2,1,0:T(8,128)(2,1)} %own_ref) | copy-start | bytes 12582916
  16.7 32.5 %copy-start.3 = (f32[1024,16]{0,1:T(8,128)S(1)}, f32[1024,16]{0,1:T(8,128)}, u32[]{:S(2)}) copy-start(f32[1024,16]{0,1:T(8,128)} %param.12) | copy-start | bytes 196612
  16.7 32.5 %copy-start.5 = (f32[1024]{0:T(1024)S(1)}, f32[1024]{0:T(1024)}, u32[]{:S(2)}) copy-start(f32[1024]{0:T(1024)} %param.11) | copy-start | bytes 12292
  16.7 58.9 %copy-start.1 = (bf16[16,4,64,128]{3,2,1,0:T(8,128)(2,1)S(1)}, bf16[16,4,64,128]{3,2,1,0:T(8,128)(2,1)}, u32[]{:S(2)}) copy-start(bf16[16,4,64,128]{3,2,1,0:T(8,128)(2,1)} %base_ref.1) | copy-start | bytes 3145732

commit v4 on v3

--- a/solution.py
+++ b/solution.py
@@ -36,7 +36,7 @@
 
 
 def stencil_kernel(
-    planes, width, modes_count, group, edge_ref, cells_ref, cells_b_ref, cells_a_ref,
+    planes, width, modes_count, group, n_slab, plan_ref,
     log_ref, slope_ref, modes_ref, own_ref, below_ref, above_ref,
     coef, gain, cond, t_ref, u_ref, r_ref,
 ):
@@ -44,8 +44,10 @@
     lanes = log_ref.shape[-1]
     pad = 8
     tiles = width // 8
-    stride = (planes + 2 * REACH) * width + pad
+    stride = pick_stride(modes_count)
     n_ext = planes + 2 * REACH + 2
+    first = lax.axis_index("slab") == 0
+    last = lax.axis_index("slab") == n_slab - 1
 
     @pl.when(step == 0)
     def _():
@@ -53,11 +55,11 @@
         for z in range(n_ext):
             cond[pl.ds(pad + z * width, width), :] = jnp.exp(log_ref[z])
 
-        @pl.when(edge_ref[0] == 1)
+        @pl.when(first)
         def _():
             cond[pl.ds(pad + 2 * width, width), :] = cond[pl.ds(pad + 3 * width, width), :]
 
-        @pl.when(edge_ref[1] == 1)
+        @pl.when(last)
         def _():
             cond[pl.ds(pad + (planes + 3) * width, width), :] = cond[
                 pl.ds(pad + (planes + 2) * width, width), :
@@ -67,8 +69,6 @@
         u_ref[...] = jnp.zeros_like(u_ref)
         rows = lax.broadcasted_iota(jnp.int32, (8, lanes), 0)
         cols = lax.broadcasted_iota(jnp.int32, (8, lanes), 1)
-        first = edge_ref[0] == 1
-        last = edge_ref[1] == 1
         for z in range(planes + 2 * REACH):
             def body(i, carry, z=z):
                 at = pad + (z + 1) * width + i * 8
@@ -108,8 +108,9 @@
                 return carry
 
             lax.fori_loop(0, tiles, body, 0, unroll=8)
-        for k in range(modes_count):
-            r_ref[pl.ds(k * stride + stride - pad, pad), :] = jnp.zeros((pad, lanes), jnp.float32)
+        r_ref[pl.ds((planes + 2 * REACH) * width * stride, modes_count), :] = jnp.zeros(
+            (modes_count, lanes), jnp.float32
+        )
 
     for z in range(planes):
         def convert(i, carry, z=z):
@@ -189,10 +190,8 @@
                     total = total + SELF_3 * centre
                     if 0 <= z < planes:
                         total = total + SOURCE_3 * t_ref[m, pl.ds(pad + z * width + i * 8, 8), :]
-                put = pl.multiple_of(
-                    (step * group + m) * stride + (z + REACH) * width + i * 8, 8
-                )
-                r_ref[pl.ds(put, 8), :] = total
+                put = ((z + REACH) * width + i * 8) * stride + step * group + m
+                r_ref[pl.ds(put, 8, stride=stride), :] = total
             return carry
 
         lax.fori_loop(0, tiles, third, 0, unroll=tiles)
@@ -200,23 +199,14 @@
     @pl.when(step == pl.num_programs(0) - 1)
     def _():
         cols = lax.broadcasted_iota(jnp.int32, (modes_count, lanes), 1)
-        count = cells_ref.shape[0]
-        zero_row = stride - pad
-        shift = lanes.bit_length() - 1
-
-        def pick(cells, out, low, high, offset):
-            def block(b, carry):
+        blocks = plan_ref.shape[1]
+        for kind, out in enumerate((own_ref, below_ref, above_ref)):
+
+            def block(b, carry, kind=kind, out=out):
                 def one(i, acc):
-                    cell = cells[b * lanes + i]
-                    row = cell >> shift
-                    lane = cell & (lanes - 1)
-                    if low is not None:
-                        inside = jnp.logical_and(row >= low, row < high)
-                        row = jnp.where(inside, row + offset, zero_row)
-                    else:
-                        row = row + offset
-                    v = r_ref[pl.ds(row, modes_count, stride=stride), :]
-                    v = pltpu.roll(v, (i - lane) & (lanes - 1), axis=1)
+                    start = pl.multiple_of(plan_ref[2 * kind, b, i], 8)
+                    v = r_ref[pl.ds(start, modes_count), :]
+                    v = pltpu.roll(v, plan_ref[2 * kind + 1, b, i], axis=1)
                     return jnp.where(cols == i, v, acc)
 
                 acc = lax.fori_loop(
@@ -225,31 +215,29 @@
                 out[:, pl.ds(pl.multiple_of(b * lanes, lanes), lanes)] = acc
                 return carry
 
-            lax.fori_loop(0, count // lanes, block, 0)
-
-        pick(cells_ref, own_ref, None, None, REACH * width)
-        pick(
-            cells_b_ref, below_ref, (planes - REACH) * width, planes * width,
-            (REACH - planes) * width,
-        )
-        pick(cells_a_ref, above_ref, 0, REACH * width, (REACH + planes) * width)
-
-
-def stencil(edges, cells, cells_b, cells_a, log_ext, slope, modes):
+            lax.fori_loop(0, blocks, block, 0)
+
+
+def pick_stride(modes_count):
+    return 8 * (pl.cdiv(modes_count, 8) | 1)
+
+
+def stencil(plan, log_ext, slope, modes):
     modes_count, planes, width, lanes = modes.shape
-    count = cells.shape[0]
+    count = plan.shape[1] * plan.shape[2]
     group = min(8, modes_count)
     n_ext = planes + 2 * REACH + 2
-    stride = (planes + 2 * REACH) * width + 8
+    stride = pick_stride(modes_count)
     smem = pl.BlockSpec(memory_space=pltpu.SMEM)
     vmem = pl.BlockSpec(memory_space=pltpu.VMEM)
     shape = jax.ShapeDtypeStruct((modes_count, count), jnp.float32)
     return pl.pallas_call(
-        functools.partial(stencil_kernel, planes, width, modes_count, group),
+        functools.partial(
+            stencil_kernel, planes, width, modes_count, group, lax.axis_size("slab")
+        ),
         grid=(modes_count // group,),
         out_shape=(shape, shape, shape),
-        in_specs=[smem] * 4
-        + [vmem, vmem, pl.BlockSpec((group, planes, width, lanes), lambda s: (s, 0, 0, 0))],
+        in_specs=[smem, vmem, vmem, pl.BlockSpec((group, planes, width, lanes), lambda s: (s, 0, 0, 0))],
         out_specs=(pl.BlockSpec((modes_count, count), lambda s: (0, 0)),) * 3,
         scratch_shapes=[
             pltpu.VMEM((planes + 2 * REACH, 6, width, lanes), jnp.float32),
@@ -257,16 +245,158 @@
             pltpu.VMEM((n_ext * width + 16, lanes), jnp.float32),
             pltpu.VMEM((group, planes * width + 16, lanes), jnp.float32),
             pltpu.VMEM((group, (planes + 2) * width + 16, lanes), jnp.float32),
-            pltpu.VMEM((modes_count * stride, lanes), jnp.float32),
+            pltpu.VMEM(((planes + 2 * REACH) * width * stride + modes_count, lanes), jnp.float32),
         ],
         compiler_params=pltpu.CompilerParams(
-            dimension_semantics=("arbitrary",), vmem_limit_bytes=46 * MIB
+            dimension_semantics=("arbitrary",), vmem_limit_bytes=61 * MIB
         ),
         cost_estimate=pl.CostEstimate(
             flops=40 * modes.size, bytes_accessed=4 * modes.size, transcendentals=0
         ),
         name="stencil",
-    )(edges, cells, cells_b, cells_a, log_ext, slope, modes)
+    )(plan, log_ext, slope, modes)
+
+
+def halo_kernel(n_mode, n_slab, stride, log_ref, cells_ref, modes_ref, ext, plan, *rest):
+    pieces = rest[: n_mode - 1]
+    cells_b, cells_a, send, recv, local = rest[n_mode - 1 :]
+    me = lax.axis_index("mode")
+    slab = lax.axis_index("slab")
+    planes, width, lanes = log_ref.shape
+    part = width // n_mode
+    halo = REACH + 1
+    has_below = slab > 0
+    has_above = slab < n_slab - 1
+    slab_up = jnp.minimum(slab + 1, n_slab - 1)
+    slab_down = jnp.maximum(slab - 1, 0)
+    barrier = pltpu.get_barrier_semaphore()
+
+    @pl.when(jnp.logical_not(has_below))
+    def _():
+        ext[:halo] = jnp.zeros((halo, width, lanes), jnp.float32)
+        cells_b[...] = jnp.zeros_like(cells_b)
+
+    @pl.when(jnp.logical_not(has_above))
+    def _():
+        ext[halo + planes :] = jnp.zeros((halo, width, lanes), jnp.float32)
+        cells_a[...] = jnp.zeros_like(cells_a)
+
+    def greet(device):
+        pl.semaphore_signal(barrier, inc=1, device_id=device, device_id_type=pl.DeviceIdType.MESH)
+
+    @pl.when(has_above)
+    def _():
+        greet((me, slab_up))
+
+    @pl.when(has_below)
+    def _():
+        greet((me, slab_down))
+
+    moves = []
+    for d in range(1, n_mode):
+        to = lax.rem(me + d, n_mode)
+        source = modes_ref.at[:, :, pl.ds(pl.multiple_of(to * part, 16), part), :]
+        moves.append(pltpu.make_async_copy(source, pieces[d - 1], local.at[d]))
+    pl.semaphore_wait(barrier, jnp.where(has_below, 1, 0) + jnp.where(has_above, 1, 0))
+
+    def remote(src, dst, k, device):
+        return pltpu.make_async_remote_copy(
+            src_ref=src, dst_ref=dst, send_sem=send.at[k], recv_sem=recv.at[k],
+            device_id=device, device_id_type=pl.DeviceIdType.MESH,
+        )
+
+    up = (
+        remote(log_ref.at[planes - halo :], ext.at[:halo], 0, (me, slab_up)),
+        remote(cells_ref, cells_b, 1, (me, slab_up)),
+    )
+    down = (
+        remote(log_ref.at[:halo], ext.at[halo + planes :], 2, (me, slab_down)),
+        remote(cells_ref, cells_a, 3, (me, slab_down)),
+    )
+
+    @pl.when(has_above)
+    def _():
+        for copy in up:
+            copy.start()
+
+    @pl.when(has_below)
+    def _():
+        for copy in down:
+            copy.start()
+
+    for move in moves:
+        move.start()
+    ext[halo : halo + planes] = log_ref[...]
+
+    @pl.when(has_below)
+    def _():
+        for copy in up:
+            copy.wait_recv()
+
+    @pl.when(has_above)
+    def _():
+        for copy in down:
+            copy.wait_recv()
+
+    column = lax.broadcasted_iota(jnp.int32, cells_ref.shape, 1)
+    zero_row = (planes + 2 * REACH) * width
+    for kind, (cells, low, high, offset) in enumerate(
+        (
+            (cells_ref, 0, planes, REACH),
+            (cells_b, planes - REACH, planes, REACH - planes),
+            (cells_a, 0, REACH, REACH + planes),
+        )
+    ):
+        cell = cells[...]
+        row = cell // lanes
+        inside = jnp.logical_and(row >= low * width, row < high * width)
+        row = jnp.where(inside, row + offset * width, zero_row)
+        plan[2 * kind] = row * stride
+        plan[2 * kind + 1] = lax.rem(column - (cell - cell // lanes * lanes) + lanes, lanes)
+
+    @pl.when(has_above)
+    def _():
+        for copy in up:
+            copy.wait_send()
+
+    @pl.when(has_below)
+    def _():
+        for copy in down:
+            copy.wait_send()
+
+    for move in moves:
+        move.wait()
+
+
+def halo(log_cond, obs_cells, modes):
+    planes, width, lanes = log_cond.shape
+    modes_count = modes.shape[0]
+    n_mode = lax.axis_size("mode")
+    n_slab = lax.axis_size("slab")
+    cells = obs_cells.reshape(-1, lanes)
+    vmem = pl.BlockSpec(memory_space=pltpu.VMEM)
+    hbm = pl.BlockSpec(memory_space=pl.ANY)
+    dma = pltpu.SemaphoreType.DMA
+    piece = jax.ShapeDtypeStruct((modes_count, planes, width // n_mode, lanes), modes.dtype)
+    return pl.pallas_call(
+        functools.partial(halo_kernel, n_mode, n_slab, pick_stride(modes_count)),
+        out_shape=(
+            jax.ShapeDtypeStruct((planes + 2 * REACH + 2, width, lanes), jnp.float32),
+            jax.ShapeDtypeStruct((6,) + cells.shape, jnp.int32),
+        )
+        + (piece,) * (n_mode - 1),
+        in_specs=[vmem, vmem, hbm],
+        out_specs=(vmem, vmem) + (hbm,) * (n_mode - 1),
+        scratch_shapes=[
+            pltpu.VMEM(cells.shape, jnp.int32),
+            pltpu.VMEM(cells.shape, jnp.int32),
+            dma((4,)), dma((4,)), dma((n_mode,)),
+        ],
+        compiler_params=pltpu.CompilerParams(
+            collective_id=1, has_side_effects=True, vmem_limit_bytes=61 * MIB
+        ),
+        name="halo",
+    )(log_cond, cells, modes)
 
 
 def eliminate(matrix, n, block=4):
@@ -360,37 +490,53 @@
             device_id=device, device_id_type=pl.DeviceIdType.MESH,
         )
 
-    going_up = remote(above, in_b, halo_send.at[0], halo_recv.at[0], (me, slab_up))
-    going_down = remote(below, in_a, halo_send.at[1], halo_recv.at[1], (me, slab_down))
-
-    @pl.when(has_above)
-    def _():
-        going_up.start()
-
-    @pl.when(has_below)
-    def _():
-        going_down.start()
-
-    @pl.when(has_below)
-    def _():
-        going_up.wait_recv()
-
-    @pl.when(has_above)
-    def _():
-        going_down.wait_recv()
-
-    picked[...] = own[...] + in_b[...] + in_a[...]
+    pieces = []
+    for d in range(n_mode):
+        to = lax.rem(me + d, n_mode)
+        pieces.append(pl.ds(pl.multiple_of(to * split, 128), split))
+    going_up = [
+        remote(above.at[:, p], in_b.at[:, p], halo_send.at[d], halo_recv.at[d], (me, slab_up))
+        for d, p in enumerate(pieces)
+    ]
+    going_down = [
+        remote(below.at[:, p], in_a.at[:, p], halo_send.at[n_mode + d], halo_recv.at[n_mode + d],
+               (me, slab_down))
+        for d, p in enumerate(pieces)
+    ]
+    order = list(range(1, n_mode)) + [0]
+    for d in order:
+
+        @pl.when(has_above)
+        def _(d=d):
+            going_up[d].start()
+
+        @pl.when(has_below)
+        def _(d=d):
+            going_down[d].start()
 
     copies = []
-    for d in range(1, n_mode):
-        to = lax.rem(me + d, n_mode)
-        piece = pl.ds(pl.multiple_of(to * split, 128), split)
-        copies.append(
-            remote(picked.at[:, piece], whole.at[me], mode_send.at[d], mode_recv.at[d], (to, slab))
-        )
-        copies[-1].start()
-    here = pl.ds(pl.multiple_of(me * split, 128), split)
-    whole[me] = picked[:, here]
+    for d in order:
+
+        @pl.when(has_below)
+        def _(d=d):
+            going_up[d].wait_recv()
+
+        @pl.when(has_above)
+        def _(d=d):
+            going_down[d].wait_recv()
+
+        p = pieces[d]
+        total = own[:, p] + in_b[:, p] + in_a[:, p]
+        if d:
+            picked[:, p] = total
+            to = lax.rem(me + d, n_mode)
+            copies.append(
+                remote(picked.at[:, p], whole.at[me], mode_send.at[d], mode_recv.at[d], (to, slab))
+            )
+            copies[-1].start()
+        else:
+            whole[me] = total
+    here = pieces[0]
     for copy in copies:
         copy.wait_recv()
     every = whole[...].reshape(n, split)
@@ -400,18 +546,21 @@
         preferred_element_type=jnp.float32,
     )
     rhs = lax.dot_general(
-        scaled, miss[:, here], (((1,), (1,)), ((), ())), precision=lax.Precision.HIGHEST,
+        miss[:, here], scaled, (((1,), (1,)), ((), ())), precision=lax.Precision.HIGHEST,
         preferred_element_type=jnp.float32,
     )
-    work[...] = jnp.zeros_like(work)
-    work[:, :n] = gram
-    work[:, n : n + f] = rhs
+    top, some = n // 2, f // 2
+    sums[0, :top, :n] = gram[:top]
+    sums[0, :top, n:] = gram[top:]
+    sums[0, top:, :n] = rhs[:some]
+    sums[0, top:, n:] = rhs[some:]
 
     base = 0
     sem = 0
     for stage in stages:
         size = stage[0] * stage[2]
-        sums[base] = work[...]
+        if base:
+            sums[base] = total
         moving = []
         for d in range(1, size):
             moving.append(
@@ -429,14 +578,18 @@
         for q in range(size):
             term = sums[base + lax.rem(low - q + size, size)]
             total = term if total is None else total + term
-        work[...] = total
         copies += moving
         base += size
 
-    matrix = work[...]
+    work[...] = jnp.zeros_like(work)
+    work[:top, :n] = total[:top, :n]
+    work[top:n, :n] = total[:top, n:]
+    work[n : n + some, :n] = total[top:, :n]
+    work[n + some : n + f, :n] = total[top:, n:]
+    matrix = work[...].T[:n]
     tall = lax.broadcasted_iota(jnp.int32, matrix.shape, 0)
     wide = lax.broadcasted_iota(jnp.int32, matrix.shape, 1)
-    work[...] = eliminate(matrix + jnp.where(tall == wide, 1.0, 0.0), n)
+    work[:n] = eliminate(matrix + jnp.where(tall == wide, 1.0, 0.0), n)
     for d in range(n_mode):
         block = lax.rem(me - d + n_mode, n_mode)
         out[d * mine : (d + 1) * mine, :] = work[
@@ -445,11 +598,13 @@
 
     @pl.when(has_above)
     def _():
-        going_up.wait_send()
+        for copy in going_up:
+            copy.wait_send()
 
     @pl.when(has_below)
     def _():
-        going_down.wait_send()
+        for copy in going_down:
+            copy.wait_send()
 
     for copy in copies:
         copy.wait_send()
@@ -476,9 +631,9 @@
             pltpu.VMEM((mine, count), jnp.float32),
             pltpu.VMEM((mine, count), jnp.float32),
             pltpu.VMEM((n_mode, mine, count // n_mode), jnp.float32),
-            pltpu.VMEM((slots, n, wide), jnp.float32),
-            pltpu.VMEM((n, wide), jnp.float32),
-            dma((2,)), dma((2,)), dma((n_mode,)), dma((n_mode,)), dma((slots,)), dma((slots,)),
+            pltpu.VMEM((slots, (n + f) // 2, 2 * n), jnp.float32),
+            pltpu.VMEM((wide, wide), jnp.float32),
+            dma((2 * n_mode,)), dma((2 * n_mode,)), dma((n_mode,)), dma((n_mode,)), dma((slots,)), dma((slots,)),
         ],
         compiler_params=pltpu.CompilerParams(
             collective_id=0, has_side_effects=True, vmem_limit_bytes=24 * MIB
@@ -575,54 +730,22 @@
         ),
         out_shape=jax.ShapeDtypeStruct(base.shape, jnp.float32),
         compiler_params=pltpu.CompilerParams(
-            dimension_semantics=("arbitrary", "arbitrary"), vmem_limit_bytes=32 * MIB
+            dimension_semantics=("arbitrary", "arbitrary"), vmem_limit_bytes=61 * MIB
         ),
         name="update",
     )(place, coef, modes, others, base)
 
 
 def on_device(log_cond, head_slope, modes, obs_cells, obs_var, misfit, base_fields):
-    planes, width, lanes = log_cond.shape
     n_mode = lax.axis_size("mode")
-    n_slab = lax.axis_size("slab")
     me = lax.axis_index("mode")
-    level = lax.axis_index("slab")
-    part = width // n_mode
-
-    up = [(i, i + 1) for i in range(n_slab - 1)]
-    down = [(i + 1, i) for i in range(n_slab - 1)]
-    halo = REACH + 1
-    cells_f = obs_cells.astype(jnp.float32).reshape(-1, lanes)
-
-    def message(planes_out):
-        return jnp.concatenate([planes_out.reshape(-1, lanes), cells_f], axis=0)
-
-    to_above, to_below, modes = lax.optimization_barrier(
-        (message(log_cond[-halo:]), message(log_cond[:halo]), modes)
-    )
-    from_below = lax.ppermute(to_above, "slab", up)
-    from_above = lax.ppermute(to_below, "slab", down)
-    received = []
-    for d in range(1, n_mode):
-        to = (me + d) % n_mode
-        piece = lax.dynamic_slice_in_dim(modes, to * part, part, axis=2)
-        received.append(
-            lax.ppermute(piece, "mode", [(i, (i + d) % n_mode) for i in range(n_mode)])
-        )
+    log_ext, plan, *pieces = halo(log_cond, obs_cells, modes)
+    received = [
+        lax.ppermute(piece, "mode", [(i, (i + d) % n_mode) for i in range(n_mode)])
+        for d, piece in enumerate(pieces, 1)
+    ]
     others = received[0] if n_mode == 2 else jnp.concatenate(received, axis=0)
-
-    log_ext = jnp.concatenate(
-        [
-            from_below[: halo * width].reshape(halo, width, lanes),
-            log_cond,
-            from_above[: halo * width].reshape(halo, width, lanes),
-        ],
-        axis=0,
-    )
-    cells_b = from_below[halo * width :].reshape(-1).astype(jnp.int32)
-    cells_a = from_above[halo * width :].reshape(-1).astype(jnp.int32)
-    edges = jnp.stack([level == 0, level == n_slab - 1]).astype(jnp.int32)
-    own, below, above = stencil(edges, obs_cells, cells_b, cells_a, log_ext, head_slope, modes)
+    own, below, above = stencil(plan, log_ext, head_slope, modes)
     coef = reduce_and_solve(own, below, above, obs_var, misfit)
     return update(me.astype(jnp.int32).reshape(1), coef, modes, others, base_fields)
 

time: 81.2 us -> 141 us (1.74)
  Pallas kernels: 64.2 us -> 133 us
  waiting for transfers between devices: 3.52 us -> 0.01 us
  starting transfers between devices: 5.69 us -> 2.62 us
  local copies, waits for them, and re-layouts: 6.53 us -> 4.65 us
    pallas_call x0 -> x1, Pallas kernels: none -> 67 us  [halo(): pl.pallas_call(functools.partial(halo_kernel, n_mode, n_slab, pick_stride...]
    ppermute x2 -> x0, waiting for transfers between devices: 3.51 us -> none  [the longest x1 3.51 us: on_device(): from_above = lax.ppermute(to_below, 'slab', down)]
    dynamic_slice x1 -> x0, local copies, waits for them, and re-layouts: 3.25 us -> none  [on_device(): piece = lax.dynamic_slice_in_dim(modes, to * part, part, axis=2)]
    ppermute x2 -> x0, starting transfers between devices: 2.75 us -> none  [the longest x1 1.46 us: on_device(): from_below = lax.ppermute(to_above, 'slab', up)]
    unnamed x14, local copies, waits for them, and re-layouts: 2.21 us -> 4.65 us
    pallas_call x1, Pallas kernels: 5.37 us -> 7.74 us  [update(): pl.pallas_call(update_kernel, grid_spec=pltpu.PrefetchScalarGridSpec(num_...]
  transfers between devices with their start and end apart: 3 -> 1, of which waited for: 1 -> 0; matrix products, arithmetic and copies ran while one was open for 0% -> 0% of each run, Pallas kernels for 73% -> 42%
where the time goes in v4:
time: 141 us
  Pallas kernels  133 us (94%)
  local copies, waits for them, and re-layouts  4.65 us (3%)
  starting transfers between devices  2.62 us (2%)
    pallas_call x1, Pallas kernels, halo(): pl.pallas_call(functools.partial(halo_kernel, n_mode, n_slab, pick_stride...  67 us
    pallas_call x1, Pallas kernels, stencil(): pl.pallas_call(functools.partial(stencil_kernel, planes, width, modes_cou...  32.5 us
    pallas_call x1, Pallas kernels, reduce_and_solve(): pl.pallas_call(functools.partial(reduce_kernel, n_mode, n_slab, stages),...  26.1 us
    pallas_call x1, Pallas kernels, update(): pl.pallas_call(update_kernel, grid_spec=pltpu.PrefetchScalarGridSpec(num_...  7.74 us
    unnamed x14, local copies, waits for them, and re-layouts  4.65 us
  transfers between devices with their start and end apart: 1, of which 0 were waited for; matrix products, arithmetic and copies ran while one was open for 0% of the time, Pallas kernels for 42%

profile of v4, /device:TPU:0, one launch (start us, length us, event | category | flops | bytes accessed | tf_op | source)
XLA Modules:
  0.0 140.7 jit_solution(4678023803258207871)
XLA Ops:
  0.0 67.0 %halo.1 = (f32[10,128,128]{2,1,0:T(8,128)}, s32[6,8,128]{2,1,0:T(8,128)}, bf16[32,4,64,128]{3,2,1,0:T(8,128)(2,1)}) custom-call(f32[4,128,128]{2,1,0:T(8,128)} %log_ref.1, s32[8,128]{1,0:T(8,128)} %bitcast.6, bf16[32,4,128,128]{3,2,1,0:T(8,128)(2,1)} %own_ref.1), custom_call_target="tpu_custom_call" | custom-call | tf_op jit(solution)/shard_map/halo/pallas_call | solution.py:381
  67.0 2.6 %collective-permute-start = (bf16[32,4,64,128]{3,2,1,0:T(8,128)(2,1)}, bf16[32,4,64,128]{3,2,1,0:T(8,128)(2,1)S(1)}, u32[]{:S(2)}, u32[]{:S(2)}) collective-permute-start(bf16[32,4,64,128]{3,2,1,0:T(8,128)(2,1)} %get-tuple-element.16), channel_id=1, source_target_pairs={{0,16},{16,0},{1,17},{17,1},{2,18},{18,2},{3,19},{19,3},{4,20},{20... | collective-permute-start | bytes 6291464 | tf_op jit(solution)/shard_map/ppermute | solution.py:744
  69.6 0.0 copy-start.4
  69.6 0.0 copy-start.5
  69.6 32.5 %stencil.1 = (f32[32,1024]{1,0:T(8,128)}, f32[32,1024]{1,0:T(8,128)}, f32[32,1024]{1,0:T(8,128)}) custom-call(s32[6,8,128]{2,1,0:T(8,128)} %get-tuple-element.11.plan_ref, f32[10,128,128]{2,1,0:T(8,128)} %get-tuple-element.12.log_ref, f32[4,128,128]{2,1,0:T(8,128)} %slope_ref.1, bf16[32,4,128,128]{3,2,1,0:T(8,128)(2,1)} %own_ref.1), custom_call_target="tpu_custom_call" | custom-call | flops 83886080 | bytes 8388608 | tf_op jit(solution)/shard_map/stencil/pallas_call | solution.py:234
  102.2 0.0 copy-done.4
  102.2 0.0 copy-done.5
  102.2 0.0 copy-start.1
  102.2 0.9 copy-done.1
  103.1 0.0 copy-start.2
  103.1 0.9 copy-done.2
  104.0 0.0 copy-start.3
  104.0 0.9 copy-done.3
  104.9 26.1 %reduce_and_solve.1.coef_ref = f32[64,16]{1,0:T(8,128)S(1)} custom-call(f32[32,1024]{1,0:T(8,128)S(1)} %copy-done.1, f32[32,1024]{1,0:T(8,128)S(1)} %copy-done.2, f32[32,1024]{1,0:T(8,128)S(1)} %copy-done.3, f32[1,1024]{1,0:T(1,128)S(1)} %bitcast.5, f32[16,1024]{1,0:T(8,128)S(1)} %bitcast.4), custom_call_target="tpu_custom_call" | custom-call | flops 8388608 | bytes 1048576 | tf_op jit(solution)/shard_map/reduce_and_solve/pallas_call | solution.py:624
  131.0 0.0 copy-start
  131.0 0.6 copy-done
  131.6 0.0 collective-permute-done.others_ref
  131.6 0.0 copy-start.6
  131.6 1.3 copy-done.6
  132.9 7.7 %update.1 = f32[16,4,64,128]{3,2,1,0:T(8,128)} custom-call(s32[1]{0:T(128)} %bitcast.place_ref, f32[64,16]{1,0:T(8,128)} %copy-done, bf16[32,4,128,128]{3,2,1,0:T(8,128)(2,1)} %own_ref.1, bf16[32,4,64,128]{3,2,1,0:T(8,128)(2,1)} %copy-done.6, bf16[16,4,64,128]{3,2,1,0:T(8,128)(2,1)} %base_ref.1), custom_call_target="tpu_custom_call" | custom-call | tf_op jit(solution)/shard_map/update/pallas_call | solution.py:712
Async XLA Ops:
  67.0 64.6 %collective-permute-start = (bf16[32,4,64,128]{3,2,1,0:T(8,128)(2,1)}, bf16[32,4,64,128]{3,2,1,0:T(8,128)(2,1)S(1)}, u32[]{:S(2)}, u32[]{:S(2)}) collective-permute-start(bf16[32,4,64,128]{3,2,1,0:T(8,128)(2,1)} %get-tuple-element.16), channel_id=1, source_target_pairs={{0,16},{16,0},{1,17},{17,1},{2,18},{18,2},{3,19},{19,3},{4,20},{20... | collective-permute-start | bytes 6291464 | tf_op jit(solution)/shard_map/ppermute | solution.py:744
  69.6 32.5 %copy-start.4 = (f32[1024,16]{0,1:T(8,128)S(1)}, f32[1024,16]{0,1:T(8,128)}, u32[]{:S(2)}) copy-start(f32[1024,16]{0,1:T(8,128)} %param.12) | copy-start | bytes 196612
  69.6 32.5 %copy-start.5 = (f32[1024]{0:T(1024)S(1)}, f32[1024]{0:T(1024)}, u32[]{:S(2)}) copy-start(f32[1024]{0:T(1024)} %param.11) | copy-start | bytes 12292
  102.2 0.9 copy-start.1
  103.1 0.9 copy-start.2
  104.0 0.9 copy-start.3
  131.0 0.6 copy-start
  131.6 1.3 copy-start.6

commit v5 on v4

--- a/solution.py
+++ b/solution.py
@@ -248,7 +248,7 @@
             pltpu.VMEM(((planes + 2 * REACH) * width * stride + modes_count, lanes), jnp.float32),
         ],
         compiler_params=pltpu.CompilerParams(
-            dimension_semantics=("arbitrary",), vmem_limit_bytes=61 * MIB
+            dimension_semantics=("arbitrary",), vmem_limit_bytes=46 * MIB
         ),
         cost_estimate=pl.CostEstimate(
             flops=40 * modes.size, bytes_accessed=4 * modes.size, transcendentals=0
@@ -386,7 +386,7 @@
         )
         + (piece,) * (n_mode - 1),
         in_specs=[vmem, vmem, hbm],
-        out_specs=(vmem, vmem) + (hbm,) * (n_mode - 1),
+        out_specs=(vmem, vmem) + (vmem,) * (n_mode - 1),
         scratch_shapes=[
             pltpu.VMEM(cells.shape, jnp.int32),
             pltpu.VMEM(cells.shape, jnp.int32),
@@ -730,7 +730,7 @@
         ),
         out_shape=jax.ShapeDtypeStruct(base.shape, jnp.float32),
         compiler_params=pltpu.CompilerParams(
-            dimension_semantics=("arbitrary", "arbitrary"), vmem_limit_bytes=61 * MIB
+            dimension_semantics=("arbitrary", "arbitrary"), vmem_limit_bytes=32 * MIB
         ),
         name="update",
     )(place, coef, modes, others, base)

time: 141 us -> 78.3 us (0.56)
  Pallas kernels: 133 us -> 72.4 us
    pallas_call x1, Pallas kernels: 67 us -> 6.71 us  [halo(): pl.pallas_call(functools.partial(halo_kernel, n_mode, n_slab, pick_stride...]
    pallas_call x1, Pallas kernels: 26.1 us -> 29.1 us  [reduce_and_solve(): pl.pallas_call(functools.partial(reduce_kernel, n_mode, n_slab, stages),...]
    pallas_call x1, Pallas kernels: 7.74 us -> 5.36 us  [update(): pl.pallas_call(update_kernel, grid_spec=pltpu.PrefetchScalarGridSpec(num_...]
  transfers between devices with their start and end apart: 1 -> 1, of which waited for: 0 -> 0; matrix products, arithmetic and copies ran while one was open for 0% -> 0% of each run, Pallas kernels for 42% -> 77%
where the time goes in v5:
time: 78.3 us; the launch traced here: 78 us
  Pallas kernels  72.4 us (92%)
  local copies, waits for them, and re-layouts  4.03 us (5%)
  starting transfers between devices  1.56 us (2%)
    pallas_call x1, Pallas kernels, stencil(): pl.pallas_call(functools.partial(stencil_kernel, planes, width, modes_cou...  31.2 us
    pallas_call x1, Pallas kernels, reduce_and_solve(): pl.pallas_call(functools.partial(reduce_kernel, n_mode, n_slab, stages),...  29.1 us
    pallas_call x1, Pallas kernels, halo(): pl.pallas_call(functools.partial(halo_kernel, n_mode, n_slab, pick_stride...  6.71 us
    pallas_call x1, Pallas kernels, update(): pl.pallas_call(update_kernel, grid_spec=pltpu.PrefetchScalarGridSpec(num_...  5.36 us
    unnamed x14, local copies, waits for them, and re-layouts  4.03 us
  transfers between devices with their start and end apart: 1, of which 0 were waited for; matrix products, arithmetic and copies ran while one was open for 0% of the time, Pallas kernels for 77%

profile of v5, /device:TPU:0, one launch (start us, length us, event | category | flops | bytes accessed | tf_op | source)
XLA Modules:
  0.0 78.0 jit_solution(1647666488465181695)
XLA Ops:
  0.0 0.0 copy-start.3
  0.0 6.7 %halo.1 = (f32[10,128,128]{2,1,0:T(8,128)}, s32[6,8,128]{2,1,0:T(8,128)}, bf16[32,4,64,128]{3,2,1,0:T(8,128)(2,1)}) custom-call(f32[4,128,128]{2,1,0:T(8,128)} %log_ref.1, s32[8,128]{1,0:T(8,128)} %bitcast.6, bf16[32,4,128,128]{3,2,1,0:T(8,128)(2,1)} %own_ref.1), custom_call_target="tpu_custom_call" | custom-call | tf_op jit(solution)/shard_map/halo/pallas_call | solution.py:381
  6.7 1.6 %collective-permute-start = (bf16[32,4,64,128]{3,2,1,0:T(8,128)(2,1)}, bf16[32,4,64,128]{3,2,1,0:T(8,128)(2,1)S(1)}, u32[]{:S(2)}, u32[]{:S(2)}) collective-permute-start(bf16[32,4,64,128]{3,2,1,0:T(8,128)(2,1)} %get-tuple-element.16), channel_id=1, source_target_pairs={{0,16},{16,0},{1,17},{17,1},{2,18},{18,2},{3,19},{19,3},{4,20},{20... | collective-permute-start | bytes 6291464 | tf_op jit(solution)/shard_map/ppermute | solution.py:744
  8.3 0.0 copy-done.3
  8.3 0.0 copy-start
  8.3 2.2 %copy-done = bf16[32,4,128,128]{3,2,1,0:T(8,128)(2,1)S(1)} copy-done((bf16[32,4,128,128]{3,2,1,0:T(8,128)(2,1)S(1)}, bf16[32,4,128,128]{3,2,1,0:T(8,128)(2,1)}, u32[]{:S(2)}) %copy-start) | copy-done | bytes 4194328
  10.5 0.0 copy-start.2
  10.5 1.1 %copy-done.2 = f32[10,128,128]{2,1,0:T(8,128)S(1)} copy-done((f32[10,128,128]{2,1,0:T(8,128)S(1)}, f32[10,128,128]{2,1,0:T(8,128)}, u32[]{:S(2)}) %copy-start.2) | copy-done | bytes 655384
  11.6 0.0 copy-start.5
  11.6 0.7 copy-done.5
  12.3 0.0 copy-start.4
  12.3 0.0 copy-start.6
  12.3 0.0 copy-start.1
  12.3 31.2 %stencil.1 = (f32[32,1024]{1,0:T(8,128)S(1)}, f32[32,1024]{1,0:T(8,128)S(1)}, f32[32,1024]{1,0:T(8,128)S(1)}) custom-call(s32[6,8,128]{2,1,0:T(8,128)S(1)} %copy-done.5, f32[10,128,128]{2,1,0:T(8,128)S(1)} %copy-done.2, f32[4,128,128]{2,1,0:T(8,128)S(1)} %copy-done.3, bf16[32,4,128,128]{3,2,1,0:T(8,128)(2,1)S(1)} %copy-done), custom_call_target="tpu_custom_call" | custom-call | flops 83886080 | bytes 8388608 | tf_op jit(solution)/shard_map/stencil/pallas_call | solution.py:234
  43.5 0.0 copy-done.4
  43.5 0.0 copy-done.6
  43.5 29.1 %reduce_and_solve.1.coef_ref = f32[64,16]{1,0:T(8,128)S(1)} custom-call(f32[32,1024]{1,0:T(8,128)S(1)} %get-tuple-element.13.own, f32[32,1024]{1,0:T(8,128)S(1)} %get-tuple-element.14.below, f32[32,1024]{1,0:T(8,128)S(1)} %get-tuple-element.15.above, f32[1,1024]{1,0:T(1,128)S(1)} %bitcast.5, f32[16,1024]{1,0:T(8,128)S(1)} %bitcast.4), custom_call_target="tpu_custom_call" | custom-call | flops 8388608 | bytes 1048576 | tf_op jit(solution)/shard_map/reduce_and_solve/pallas_call | solution.py:624
  72.6 0.0 collective-permute-done.others_ref
  72.6 0.0 copy-done.1
  72.6 5.4 %update.1 = f32[16,4,64,128]{3,2,1,0:T(8,128)} custom-call(s32[1]{0:T(128)} %bitcast.place_ref, f32[64,16]{1,0:T(8,128)S(1)} %reduce_and_solve.1.coef_ref, bf16[32,4,128,128]{3,2,1,0:T(8,128)(2,1)S(1)} %copy-done, bf16[32,4,64,128]{3,2,1,0:T(8,128)(2,1)S(1)} %collective-permute-done.others_ref, bf16[16,4,64,128]{3,2,1,0:T(8,128)(2,1)S(1)} %copy-done.1), custom_call_target="tpu_custom_call" | custom-call | tf_op jit(solution)/shard_map/update/pallas_call | solution.py:712
Async XLA Ops:
  0.0 8.3 %copy-start.3 = (f32[4,128,128]{2,1,0:T(8,128)S(1)}, f32[4,128,128]{2,1,0:T(8,128)}, u32[]{:S(2)}) copy-start(f32[4,128,128]{2,1,0:T(8,128)} %slope_ref.1) | copy-start | bytes 786436
  6.7 65.9 %collective-permute-start = (bf16[32,4,64,128]{3,2,1,0:T(8,128)(2,1)}, bf16[32,4,64,128]{3,2,1,0:T(8,128)(2,1)S(1)}, u32[]{:S(2)}, u32[]{:S(2)}) collective-permute-start(bf16[32,4,64,128]{3,2,1,0:T(8,128)(2,1)} %get-tuple-element.16), channel_id=1, source_target_pairs={{0,16},{16,0},{1,17},{17,1},{2,18},{18,2},{3,19},{19,3},{4,20},{20... | collective-permute-start | bytes 6291464 | tf_op jit(solution)/shard_map/ppermute | solution.py:744
  8.3 2.2 %copy-start = (bf16[32,4,128,128]{3,2,1,0:T(8,128)(2,1)S(1)}, bf16[32,4,128,128]{3,2,1,0:T(8,128)(2,1)}, u32[]{:S(2)}) copy-start(bf16[32,4,128,128]{3,2,1,0:T(8,128)(2,1)} %own_ref.1) | copy-start | bytes 12582916
  10.5 1.1 %copy-start.2 = (f32[10,128,128]{2,1,0:T(8,128)S(1)}, f32[10,128,128]{2,1,0:T(8,128)}, u32[]{:S(2)}) copy-start(f32[10,128,128]{2,1,0:T(8,128)} %get-tuple-element.12.log_ref) | copy-start | bytes 1966084
  11.6 0.7 copy-start.5
  12.3 31.2 %copy-start.4 = (f32[1024,16]{0,1:T(8,128)S(1)}, f32[1024,16]{0,1:T(8,128)}, u32[]{:S(2)}) copy-start(f32[1024,16]{0,1:T(8,128)} %param.12) | copy-start | bytes 196612
  12.3 31.2 %copy-start.6 = (f32[1024]{0:T(1024)S(1)}, f32[1024]{0:T(1024)}, u32[]{:S(2)}) copy-start(f32[1024]{0:T(1024)} %param.11) | copy-start | bytes 12292
  12.3 60.3 %copy-start.1 = (bf16[16,4,64,128]{3,2,1,0:T(8,128)(2,1)S(1)}, bf16[16,4,64,128]{3,2,1,0:T(8,128)(2,1)}, u32[]{:S(2)}) copy-start(bf16[16,4,64,128]{3,2,1,0:T(8,128)(2,1)} %base_ref.1) | copy-start | bytes 3145732
